TPU v7x, 32 devices: a whole 2x2x4 slice. The times are simulated.
32 devices in a mesh: batch: 8 (over z, x), rep: 4 (over y, core).
Axes of the slice: x: 2, y: 2, z: 4, core: 2. Of those that a mesh axis runs over, the one named last changes fastest.
Arguments:
- tokens: bfloat16 [32, 1024, 1024], P(('batch', 'rep')), may hold values from -6 to 6
- ln1_gain: bfloat16 [1024], replicated, may hold values from 0.099609375 to 1.8984375
- ln1_shift: bfloat16 [1024], replicated, may hold values from -3 to 3
- qkv_weight: bfloat16 [1024, 3072], replicated, may hold values from -0.1875 to 0.1875
- qkv_bias: bfloat16 [3072], replicated, may hold values from -1.75 to 1.75
- out_weight: bfloat16 [1024, 1024], replicated, may hold values from -1.5 to 1.5
- out_bias: bfloat16 [1024], replicated, may hold values from -1.75 to 1.75
- ln2_gain: bfloat16 [1024], replicated, may hold values from 0.099609375 to 1.8984375
- ln2_shift: bfloat16 [1024], replicated, may hold values from -3 to 3
- fc_weight: bfloat16 [1024, 4096], replicated, may hold values from -0.1875 to 0.1875
- fc_bias: bfloat16 [4096], replicated, may hold values from -1.75 to 1.75
- proj_weight: bfloat16 [4096, 1024], replicated, may hold values from -0.09375 to 0.09375
- proj_bias: bfloat16 [1024], replicated, may hold values from -1.75 to 1.75
- prefix_embed: bfloat16 [10, 1024], replicated, may hold values from -6 to 6
- reparam_in: bfloat16 [1024, 512], replicated, may hold values from -0.1875 to 0.1875
- reparam_in_bias: bfloat16 [512], replicated, may hold values from -3 to 3
- reparam_out: bfloat16 [512, 2048], P(None, 'rep'), may hold values from -0.375 to 0.375
- reparam_out_bias: bfloat16 [2048], P('rep'), may hold values from -1.75 to 1.75
- bucket: int32 [32], P(('batch', 'rep')), may hold values from 256 to 1024, as said below
- seg_lens: int32 [32, 4], P(('batch', 'rep')), may hold values from 128 to 256, as said below
- cotangent: bfloat16 [32, 1024, 1024], P(('batch', 'rep')), may hold values from -6 to 6
Outputs:
- block_out: bfloat16 [32, 1024, 1024], P(('batch', 'rep'))
- tokens_grad: bfloat16 [32, 1024, 1024], P(('batch', 'rep'))
- embed_grad: float32 [10, 1024], replicated
- reparam_in_grad: float32 [1024, 512], replicated
- reparam_in_bias_grad: float32 [512], replicated
- reparam_out_grad: float32 [512, 2048], P(None, 'rep')
- reparam_out_bias_grad: float32 [2048], P('rep')
Inputs may be any that keep to these rules, and one draw needn't show every extreme that they name: `bucket`: each entry is 256 or 1024; both occur in every draw. `seg_lens`: in a row of bucket 256 entry j is the live length of the j-th 256-slot bucket; in a row of bucket 1024 the sum of the row's entries is the live length of its one sequence. Some entry equals 256.
All inputs are finite; a program needn't handle non-finite values.
Results may differ from a plain program's by a relative error of at most 0.015.
Values may be sent and summed in bfloat16 or wider, within the bound.
No kernel may reach another device: no remote copies, remote signals or barrier semaphores. Data moves between devices by JAX's collectives and lax.ppermute only.
A program may use at most 384 MiB of HBM per device.

v0:
```python
import jax
import jax.numpy as jnp
from jax import lax
from jax.experimental import pallas as pl
from jax.experimental.pallas import tpu as pltpu
from jax.sharding import PartitionSpec as P

D = 1024
HEADS = 16
HEAD_DIM = 64
FF = 4096
PREFIX = 10
PAD = 16
SHORT = 256
BLK = 256
QUAD = 4 * HEAD_DIM
QUADS = HEADS // 4
CHUNK = 1024

BF = jnp.bfloat16
F32 = jnp.float32
norm_eps = 1e-05
gelu_coef = 0.7978845608028654
gelu_cube = 0.044715
masked_score = -1e30


def dot_nn(left, right):
    return jnp.dot(left, right, preferred_element_type=F32)


def dot_nt(left, right):
    return lax.dot_general(left, right, (((1,), (1,)), ((), ())), preferred_element_type=F32)


def dot_tn(left, right):
    return lax.dot_general(left, right, (((0,), (0,)), ((), ())), preferred_element_type=F32)


def normalise(values):
    row_mean = jnp.mean(values, axis=-1, keepdims=True)
    centred = values - row_mean
    variance = jnp.mean(centred * centred, axis=-1, keepdims=True)
    inv = lax.rsqrt(variance + norm_eps)
    return centred * inv, inv


def norm_back(grad, norm, inv):
    along = jnp.mean(grad * norm, axis=-1, keepdims=True)
    return (grad - jnp.mean(grad, axis=-1, keepdims=True) - norm * along) * inv


def gelu_pair(u):
    sq = u * u
    w = jnp.tanh(u * (gelu_coef + (gelu_coef * gelu_cube) * sq))
    a = 0.5 * w + 0.5
    slope = a * (1.0 + u * (1.0 - a) * (2.0 * gelu_coef + (6.0 * gelu_coef * gelu_cube) * sq))
    return u * a, slope


def head_mask(shape, head):
    lane = lax.broadcasted_iota(jnp.int32, shape, 1)
    return (lane < HEAD_DIM) if head % 2 == 0 else (lane >= HEAD_DIM)


def quad_prefix(prefix, quad):
    row = lax.broadcasted_iota(jnp.int32, (128, QUAD), 0) // PAD
    col = lax.broadcasted_iota(jnp.int32, (128, QUAD), 1) // HEAD_DIM
    tiled = jnp.concatenate([prefix] * 8, axis=0)
    return jnp.where(row == col + 4 * (quad % 2), tiled, jnp.zeros_like(tiled))


def full_prefix(prefix):
    shape = (HEADS * PAD, D)
    row = lax.broadcasted_iota(jnp.int32, shape, 0) // PAD
    col = lax.broadcasted_iota(jnp.int32, shape, 1) // HEAD_DIM
    tiled = jnp.concatenate([prefix] * HEADS, axis=0)
    return jnp.where(row == col, tiled, jnp.zeros_like(tiled))


def row_of(ref, first=0, size=None):
    size = ref.shape[0] if size is None else size
    return ref[first : first + size].astype(F32)[None, :]


def padded_embed(embed_ref, pad_ref):
    pad_ref[...] = jnp.zeros_like(pad_ref)
    pad_ref[0:PREFIX, :] = embed_ref[...].astype(F32)
    return pad_ref[...].astype(BF)


def reparam_kernel(embed_ref, in_w_ref, in_b_ref, out_w_ref, out_b_ref, tanh_ref, kv_ref, pad_ref):
    tanh_pre = jnp.tanh(dot_nn(padded_embed(embed_ref, pad_ref), in_w_ref[...]) + row_of(in_b_ref))
    tanh_ref[...] = tanh_pre
    kv_ref[...] = (dot_nn(tanh_pre.astype(BF), out_w_ref[...]) + row_of(out_b_ref)).astype(BF)


def project_kernel(x_ref, gain_ref, shift_ref, bias_ref, w_ref, out_ref, normed_ref):
    step = pl.program_id(0)
    slots = x_ref.shape[0]
    factor = jnp.where(step == 0, HEAD_DIM**-0.5, 1.0)

    def norm_part(first):
        norm, _ = normalise(x_ref[first : first + BLK, :].astype(F32))
        normed_ref[first : first + BLK, :] = (norm * row_of(gain_ref) + row_of(shift_ref)).astype(BF)

    def dot_part(first, rows):
        mixed = dot_nn(normed_ref[first : first + rows, :], w_ref[...]) + row_of(bias_ref)
        out_ref[first : first + rows, :] = (mixed.astype(BF).astype(F32) * factor).astype(BF)

    @pl.when(step == 0)
    def _():
        norm_part(0)
        for first in range(0, slots, BLK):
            if first + BLK < slots:
                norm_part(first + BLK)
            dot_part(first, BLK)

    @pl.when(step > 0)
    def _():
        for first in range(0, slots, 2 * BLK):
            dot_part(first, 2 * BLK)


def live_column(bucket_ref, lens_ref, first, rows, slots):
    position = lax.broadcasted_iota(jnp.int32, (rows, 1), 0) + first
    segment = position // SHORT
    total = jnp.int32(0)
    short_len = jnp.zeros((rows, 1), jnp.int32)
    for index in range(slots // SHORT):
        total = total + lens_ref[0, index]
        short_len = jnp.where(segment == index, lens_ref[0, index], short_len)
    return position < jnp.where(bucket_ref[0] == slots, total, segment * SHORT + short_len)


def attend(q_ref, k_ref, v_ref, prefix_ref, att_ref, pp_ref, lse_ref, quad, long_row):
    slots = q_ref.shape[0]
    blocks = slots // BLK
    cols = pl.ds(pl.multiple_of(quad * QUAD, QUAD), QUAD)
    pair_cols = pl.ds(pl.multiple_of((quad // 2) * 128, 128), 128)
    prefix_keys = quad_prefix(prefix_ref[:, cols], quad)
    prefix_vals = quad_prefix(prefix_ref[:, pl.ds(pl.multiple_of(D + quad * QUAD, QUAD), QUAD)], quad)
    causal = lax.broadcasted_iota(jnp.int32, (BLK, BLK), 1) <= lax.broadcasted_iota(jnp.int32, (BLK, BLK), 0)
    lane = lax.broadcasted_iota(jnp.int32, (BLK, 128), 1)
    lane_head = lane // PAD - 4 * (quad % 2)
    lane_real = lane % PAD < PREFIX

    def keys_of(block):
        return (0 if long_row else block * BLK), (block + 1) * BLK

    def scores(block, head):
        first, last = keys_of(block)
        pair = slice(128 * (head // 2), 128 * (head // 2) + 128)
        queries = q_ref[block * BLK : (block + 1) * BLK, pair]
        queries = jnp.where(head_mask((BLK, 128), head), queries, jnp.zeros_like(queries))
        raw = dot_nt(queries, k_ref[first:last, pair])
        own = jnp.where(causal, raw[:, -BLK:], masked_score)
        return own if last - first == BLK else jnp.concatenate([raw[:, :-BLK], own], axis=1)

    units = [(block, head) for block in range(blocks) for head in range(4)]
    ahead = 2
    queue = [scores(*unit) for unit in units[:ahead]]
    for index, (block, head) in enumerate(units):
        if index + ahead < len(units):
            queue.append(scores(*units[index + ahead]))
        rows = slice(block * BLK, (block + 1) * BLK)
        if head == 0:
            prefix_raw = dot_nt(q_ref[rows, :], prefix_keys)
            probs_quad = jnp.zeros((BLK, 128), F32)
            lse_quad = jnp.zeros((BLK, 128), F32)
            outs = []
        first, last = keys_of(block)
        pair = slice(128 * (head // 2), 128 * (head // 2) + 128)
        prefix_scores = jnp.where((lane_head == head) & lane_real, prefix_raw, masked_score)
        score = jnp.concatenate([queue[index], prefix_scores], axis=1)
        queue[index] = None
        peak = jnp.max(score, axis=1, keepdims=True)
        raised = jnp.exp(score - peak)
        summed = jnp.sum(raised, axis=1, keepdims=True)
        inv = 1.0 / summed
        outs.append(dot_nn(raised[:, : last - first].astype(BF), v_ref[first:last, pair]) * inv)
        probs_quad = probs_quad + raised[:, last - first :] * inv
        lse_quad = jnp.where(lane_head == head, peak + jnp.log(summed), lse_quad)
        if head == 3:
            probs_low = probs_quad.astype(BF)
            left = head_mask((BLK, 128), 0)
            merged = jnp.concatenate(
                [jnp.where(left, outs[0], outs[1]), jnp.where(left, outs[2], outs[3])], axis=1
            ) + dot_nn(probs_low, prefix_vals)
            att_ref[rows, cols] = merged.astype(BF)

            @pl.when(quad % 2 == 0)
            def _():
                pp_ref[rows, pair_cols] = probs_low
                lse_ref[rows, pair_cols] = lse_quad

            @pl.when(quad % 2 == 1)
            def _():
                pp_ref[rows, pair_cols] = pp_ref[rows, pair_cols] + probs_low
                lse_ref[rows, pair_cols] = lse_ref[rows, pair_cols] + lse_quad


def forward_kernel(
    place_ref, bucket_ref, lens_ref, q_ref, k_ref, v_ref, x_ref, cot_ref, q_rows_ref,
    out_b_ref, gain_ref, shift_ref, fc_b_ref, proj_b_ref, out_w_hbm, fc_w_hbm, proj_w_hbm, *refs,
):
    pieces, refs = refs[: len(refs) - 28], refs[len(refs) - 28 :]
    (
        block_ref, d_mid_ref, d_att_ref, d_sp_ref, lse_t_ref, delta_t_ref, prefix_row_ref, prefix_ref,
        att_ref, pp_ref, lse_ref, out_w_ref, fc_w_ref, proj_w_ref, norm_ref, inv_ref, normed_ref, grad_out_ref,
        acc_ref, d_acc_ref, pre_ref, d_act_ref, bias_ref, vp_ref, spread_ref, d_kp_ref, d_vp_ref, sems,
    ) = refs
    step = pl.program_id(0)
    slots = q_ref.shape[0]
    copies = [
        pltpu.make_async_copy(out_w_hbm, out_w_ref, sems.at[0]),
        pltpu.make_async_copy(fc_w_hbm, fc_w_ref, sems.at[1]),
        pltpu.make_async_copy(proj_w_hbm, proj_w_ref, sems.at[2]),
    ]
    long_row = bucket_ref[0] == slots

    @pl.when(step == 0)
    def _():
        for copy in copies:
            copy.start()
        width = pieces[0].shape[1]
        for shift, piece in enumerate(pieces):
            owner = (place_ref[0] + (len(pieces) - shift)) % len(pieces)
            prefix_ref[:, pl.ds(pl.multiple_of(owner * width, 128), width)] = piece[...]
        vp_ref[...] = full_prefix(prefix_ref[:, D:])
        row = lax.broadcasted_iota(jnp.int32, (D, HEADS * PAD), 0) // HEAD_DIM
        col = lax.broadcasted_iota(jnp.int32, (D, HEADS * PAD), 1) // PAD
        spread_ref[...] = jnp.where(row == col, 1.0, 0.0).astype(BF)
        bias_ref[...] = row_of(fc_b_ref)
        d_kp_ref[...] = jnp.zeros_like(d_kp_ref)
        d_vp_ref[...] = jnp.zeros_like(d_vp_ref)

    @pl.when((step < QUADS) & long_row)
    def _():
        attend(q_ref, k_ref, v_ref, prefix_ref, att_ref, pp_ref, lse_ref, step, True)

    @pl.when((step < QUADS) & jnp.logical_not(long_row))
    def _():
        attend(q_ref, k_ref, v_ref, prefix_ref, att_ref, pp_ref, lse_ref, step, False)

    blocks = slots // BLK
    chunks = FF // CHUNK

    @pl.when(step == QUADS)
    def _():
        copies[0].wait()

    @pl.when((step >= QUADS) & (step < QUADS + blocks))
    def _():
        first = pl.multiple_of((step - QUADS) * BLK, BLK)
        rows = pl.ds(first, BLK)
        mid = x_ref[...].astype(F32) + dot_nn(att_ref[rows, :], out_w_ref[...]) + row_of(out_b_ref)
        norm, inv = normalise(mid)
        norm_ref[rows, :] = norm.astype(BF)
        inv_ref[rows, :] = inv
        normed_ref[rows, :] = (norm * row_of(gain_ref) + row_of(shift_ref)).astype(BF)
        live = live_column(bucket_ref, lens_ref, first, BLK, slots)
        grad_out_ref[rows, :] = jnp.where(live, cot_ref[...].astype(F32), 0.0).astype(BF)
        acc_ref[rows, :] = mid + row_of(proj_b_ref)

    def opened(block, chunk):
        rows = pl.ds(pl.multiple_of(block * BLK, BLK), BLK)
        part = pl.ds(pl.multiple_of(chunk * CHUNK, CHUNK), CHUNK)
        pre = dot_nn(normed_ref[rows, :], fc_w_ref[:, part]) + bias_ref[:, part]
        return pre, dot_nt(grad_out_ref[rows, :], proj_w_ref[part, :])

    @pl.when(step == QUADS + blocks)
    def _():
        copies[1].wait()
        copies[2].wait()
        pre_ref[...], d_act_ref[...] = opened(jnp.int32(0), jnp.int32(0))

    @pl.when(step >= QUADS + blocks)
    def _():
        block = step - QUADS - blocks
        rows = pl.ds(pl.multiple_of(block * BLK, BLK), BLK)
        d_acc_ref[...] = jnp.zeros_like(d_acc_ref)

        def chunk_step(chunk, carry):
            pre, d_act = pre_ref[...], d_act_ref[...]
            wraps = chunk == chunks - 1
            following = opened(
                jnp.where(wraps, jnp.minimum(block + 1, blocks - 1), block), jnp.where(wraps, 0, chunk + 1)
            )
            part = pl.ds(pl.multiple_of(chunk * CHUNK, CHUNK), CHUNK)
            act, slope = gelu_pair(pre)
            acc_ref[rows, :] += dot_nn(act.astype(BF), proj_w_ref[part, :])
            d_acc_ref[...] += dot_nt((d_act * slope).astype(BF), fc_w_ref[:, part])
            pre_ref[...], d_act_ref[...] = following
            return carry

        lax.fori_loop(0, chunks, chunk_step, 0)
        live = live_column(bucket_ref, lens_ref, block * BLK, BLK, slots)
        block_ref[...] = jnp.where(live, acc_ref[rows, :], 0.0).astype(BF)
        d_mid = grad_out_ref[rows, :].astype(F32) + norm_back(
            d_acc_ref[...] * row_of(gain_ref), norm_ref[rows, :].astype(F32), inv_ref[rows, :]
        )
        d_mid_ref[...] = d_mid
        d_att = dot_nt(d_mid.astype(BF), out_w_ref[...]).astype(BF)
        d_att_ref[...] = d_att
        product = (d_att.astype(F32) * att_ref[rows, :].astype(F32)).astype(BF)
        delta = dot_nn(product, spread_ref[...])
        probs = pp_ref[rows, :]
        d_sp = (probs.astype(F32) * (dot_nt(d_att, vp_ref[...]) - delta)).astype(BF)
        d_sp_ref[...] = d_sp
        d_kp_ref[...] += dot_tn(d_sp, q_rows_ref[...])
        d_vp_ref[...] += dot_tn(probs, d_att)
        lse_t_ref[...] = lse_ref[rows, :].T
        delta_t_ref[...] = delta.T

    @pl.when(step == pl.num_programs(0) - 1)
    def _():
        shape = (HEADS * PAD, D)
        own = (
            lax.broadcasted_iota(jnp.int32, shape, 0) // PAD
            == lax.broadcasted_iota(jnp.int32, shape, 1) // HEAD_DIM
        )
        for index, ref in enumerate((d_kp_ref, d_vp_ref)):
            kept = jnp.where(own, ref[...], 0.0)
            total = kept[0:PAD, :]
            for head in range(1, HEADS):
                total = total + kept[head * PAD : (head + 1) * PAD, :]
            prefix_row_ref[:, index * D : (index + 1) * D] = total.astype(BF)


def attend_back(
    q_ref, k_ref, v_ref, do_ref, pk_ref, dsp_ref, lse_ref, delta_ref, mix_ref, pair, long_row
):
    slots = q_ref.shape[0]
    blocks = slots // BLK
    causal = lax.broadcasted_iota(jnp.int32, (BLK, BLK), 0) <= lax.broadcasted_iota(jnp.int32, (BLK, BLK), 1)
    left = head_mask((BLK, 128), 0)
    row = lax.broadcasted_iota(jnp.int32, (128, 128), 0) // PAD
    col = lax.broadcasted_iota(jnp.int32, (128, 128), 1) // HEAD_DIM
    tiled = jnp.concatenate([pk_ref[...]] * 8, axis=0)
    prefix_keys = jnp.where(row == col + 2 * (pair % 4), tiled, jnp.zeros_like(tiled))

    def keys_of(block):
        return (0 if long_row else block * BLK), (block + 1) * BLK

    def opened(block, side):
        first, last = keys_of(block)
        rows = slice(block * BLK, (block + 1) * BLK)
        mask = head_mask((BLK, 128), side)
        queries, d_out = q_ref[rows, :], do_ref[rows, :]
        raw = dot_nt(k_ref[first:last, :], jnp.where(mask, queries, jnp.zeros_like(queries)))
        d_prob = dot_nt(v_ref[first:last, :], jnp.where(mask, d_out, jnp.zeros_like(d_out)))
        own = jnp.where(causal, raw[-BLK:], masked_score)
        return (own if last - first == BLK else jnp.concatenate([raw[:-BLK], own], axis=0)), d_prob

    units = [(block, side) for block in range(blocks) for side in range(2)]
    ahead = 2
    queue = [opened(*unit) for unit in units[:ahead]]
    d_keys = [[None] * blocks for _ in range(2)]
    d_vals = [[None] * blocks for _ in range(2)]
    d_queries = [None, None]
    for index, (block, side) in enumerate(units):
        if index + ahead < len(units):
            queue.append(opened(*units[index + ahead]))
        score, d_prob = queue[index]
        queue[index] = None
        first, last = keys_of(block)
        rows = slice(block * BLK, (block + 1) * BLK)
        stat = slice(side * PAD, side * PAD + 1)
        prob = jnp.exp(score - lse_ref[stat, rows])
        d_score = (prob * (d_prob - delta_ref[stat, rows])).astype(BF)
        d_queries[side] = dot_tn(d_score, k_ref[first:last, :])
        d_key = dot_nn(d_score, q_ref[rows, :])
        d_val = dot_nn(prob.astype(BF), do_ref[rows, :])
        for place, key_block in enumerate(range(first // BLK, last // BLK)):
            part = slice(place * BLK, (place + 1) * BLK)
            for sums, value in ((d_keys, d_key), (d_vals, d_val)):
                so_far = sums[side][key_block]
                sums[side][key_block] = value[part] if so_far is None else so_far + value[part]
        if side == 1:
            d_query = jnp.where(left, d_queries[0], d_queries[1]) + dot_nn(dsp_ref[rows, :], prefix_keys)
            mix_ref[0, rows, :] = (d_query * HEAD_DIM**-0.5).astype(BF)
    for block in range(blocks):
        rows = slice(block * BLK, (block + 1) * BLK)
        mix_ref[1, rows, :] = jnp.where(left, d_keys[0][block], d_keys[1][block]).astype(BF)
        mix_ref[2, rows, :] = jnp.where(left, d_vals[0][block], d_vals[1][block]).astype(BF)


def attend_back_kernel(bucket_ref, q_ref, *refs):
    args = (q_ref, *refs, pl.program_id(0))
    long_row = bucket_ref[0] == q_ref.shape[0]

    @pl.when(long_row)
    def _():
        attend_back(*args, True)

    @pl.when(jnp.logical_not(long_row))
    def _():
        attend_back(*args, False)


def project_back_kernel(d_mix_ref, w_ref, gain_ref, x_hbm, d_mid_hbm, grad_ref, acc_ref, x_ref, d_mid_ref, sems):
    step = pl.program_id(0)
    last = pl.num_programs(0) - 1
    slots = x_ref.shape[0]
    copies = [
        pltpu.make_async_copy(x_hbm, x_ref, sems.at[0]),
        pltpu.make_async_copy(d_mid_hbm, d_mid_ref, sems.at[1]),
    ]

    @pl.when(step == 0)
    def _():
        for copy in copies:
            copy.start()
        acc_ref[...] = dot_nt(d_mix_ref[0], w_ref[...])

    @pl.when((step > 0) & (step < last))
    def _():
        acc_ref[...] += dot_nt(d_mix_ref[0], w_ref[...])

    @pl.when(step == last)
    def _():
        for copy in copies:
            copy.wait()
        for first in range(0, slots, BLK):
            rows = slice(first, first + BLK)
            d_normed = acc_ref[rows, :] + dot_nt(d_mix_ref[0, rows, :], w_ref[...])
            norm, inv = normalise(x_ref[rows, :].astype(F32))
            back = norm_back(d_normed * row_of(gain_ref), norm, inv)
            grad_ref[rows, :] = (d_mid_ref[rows, :] + back).astype(BF)


def summed_in_order(place, pieces, ordered_ref):
    for shift, piece in enumerate(pieces):
        ordered_ref[(place + (len(pieces) - shift)) % len(pieces)] = piece[...]
    total = ordered_ref[0].astype(F32)
    for owner in range(1, len(pieces)):
        total = total + ordered_ref[owner].astype(F32)
    return total


def tail_kernel(place_ref, tanh_ref, embed_ref, in_w_ref, *refs):
    count = (len(refs) - 9) // 2
    weights, pieces = refs[:count], refs[count : 2 * count]
    (
        embed_grad_ref, in_grad_ref, in_bias_ref, out_grad_ref, out_bias_ref,
        pad_ref, ordered_ref, sum_ref, parts_ref,
    ) = refs[2 * count :]
    tanh_pre = tanh_ref[...]
    sum_ref[...] = summed_in_order(place_ref[0], pieces, ordered_ref).astype(BF)
    width = out_grad_ref.shape[1]
    for shift, weight in enumerate(weights):
        owner = (place_ref[0] + (count - shift)) % count
        own_cols = sum_ref[:, pl.ds(pl.multiple_of(owner * width, 128), width)]
        parts_ref[owner] = dot_nt(own_cols, weight[...])
        if shift == 0:
            out_grad_ref[...] = dot_tn(tanh_pre.astype(BF), own_cols)
            out_bias_ref[...] = jnp.sum(own_cols.astype(F32), axis=0, keepdims=True)
    d_hidden = parts_ref[0]
    for owner in range(1, count):
        d_hidden = d_hidden + parts_ref[owner]
    d_pre = (d_hidden * (1.0 - tanh_pre * tanh_pre)).astype(BF)
    in_grad_ref[...] = dot_tn(padded_embed(embed_ref, pad_ref), d_pre)
    in_bias_ref[...] = jnp.sum(d_pre.astype(F32), axis=0, keepdims=True)
    embed_grad_ref[...] = dot_nt(d_pre, in_w_ref[...])[0:PREFIX]


SMEM = pl.BlockSpec(memory_space=pltpu.SMEM)
ANY = pl.BlockSpec(memory_space=pl.ANY)


def params(mib):
    return pltpu.CompilerParams(vmem_limit_bytes=mib * 2**20, dimension_semantics=("arbitrary",))


def cost(flops, moved):
    return pl.CostEstimate(flops=int(flops), bytes_accessed=int(moved), transcendentals=0)


def shape(dims, dtype):
    return jax.ShapeDtypeStruct(dims, dtype)


def whole(array):
    return pl.BlockSpec(array.shape, lambda g: (0,) * len(array.shape))


def to_all(value, axis):
    size = lax.axis_size(axis)
    return [value] + [
        lax.ppermute(value, axis, [(place, (place + shift) % size) for place in range(size)])
        for shift in range(1, size)
    ]


def local(
    tokens, ln1_gain, ln1_shift, qkv_weight, qkv_bias, out_weight, out_bias, ln2_gain, ln2_shift, fc_weight,
    fc_bias, proj_weight, proj_bias, prefix_embed, reparam_in, reparam_in_bias, reparam_out, reparam_out_bias,
    bucket, seg_lens, cotangent,
):
    x, cot = tokens[0], cotangent[0]
    slots = x.shape[0]
    blocks = slots // BLK
    own_width = reparam_out.shape[1]
    hidden_width = reparam_in.shape[1]
    rep_place = lax.axis_index("rep").astype(jnp.int32)[None]

    reparam_args = (prefix_embed, reparam_in, reparam_in_bias, reparam_out, reparam_out_bias)
    reparam_outs = (shape((PAD, hidden_width), F32), shape((PAD, own_width), BF))
    tanh_pre, own_kv = pl.pallas_call(
        reparam_kernel,
        grid=(1,),
        out_shape=reparam_outs,
        in_specs=[whole(arg) for arg in reparam_args],
        out_specs=tuple(whole(out) for out in reparam_outs),
        scratch_shapes=[pltpu.VMEM((PAD, D), F32)],
        compiler_params=params(60),
        name="reparam",
    )(*reparam_args)
    prefix_pieces = to_all(own_kv, "rep")

    mixed = pl.pallas_call(
        project_kernel,
        grid=(3,),
        out_shape=shape((slots, 3 * D), BF),
        in_specs=[
            whole(x), whole(ln1_gain), whole(ln1_shift),
            pl.BlockSpec((D,), lambda n: (n,)),
            pl.BlockSpec((D, D), lambda n: (0, n)),
        ],
        out_specs=pl.BlockSpec((slots, D), lambda n: (0, n)),
        scratch_shapes=[pltpu.VMEM((slots, D), BF)],
        compiler_params=params(60),
        cost_estimate=cost(6 * slots * D * D, 16 * 2**20),
        name="project",
    )(x, ln1_gain, ln1_shift, qkv_bias, qkv_weight)
    late_weight, _ = lax.optimization_barrier((reparam_out, mixed))
    weight_pieces = to_all(late_weight, "rep")

    def quad_at(offset):
        return pl.BlockSpec((slots, QUAD), lambda g: (0, offset + jnp.minimum(g, QUADS - 1)))

    def block_of(width, start):
        return pl.BlockSpec((BLK, width), lambda g: (jnp.clip(g - start, 0, blocks - 1), 0))

    lanes = HEADS * PAD
    late = QUADS + blocks
    block_t = pl.BlockSpec((lanes, BLK), lambda g: (0, jnp.clip(g - late, 0, blocks - 1)))
    vectors = (out_bias, ln2_gain, ln2_shift, fc_bias, proj_bias)
    prefix_shape = shape((PAD, 2 * D), BF)
    block_out, d_mid, d_att, d_sp, lse_t, delta_t, prefix_row, prefix_kv = pl.pallas_call(
        forward_kernel,
        grid=(QUADS + 2 * blocks,),
        out_shape=(
            shape((slots, D), BF),
            shape((slots, D), F32),
            shape((slots, D), BF),
            shape((slots, lanes), BF),
            shape((lanes, slots), F32),
            shape((lanes, slots), F32),
            prefix_shape,
            prefix_shape,
        ),
        in_specs=[
            SMEM, SMEM, SMEM, quad_at(0), quad_at(QUADS), quad_at(2 * QUADS),
            block_of(D, QUADS), block_of(D, QUADS), block_of(D, late),
            *[whole(vector) for vector in vectors], ANY, ANY, ANY, *[whole(piece) for piece in prefix_pieces],
        ],
        out_specs=(
            block_of(D, late), block_of(D, late), block_of(D, late), block_of(lanes, late), block_t, block_t,
            whole(prefix_shape), whole(prefix_shape),
        ),
        scratch_shapes=[
            pltpu.VMEM((slots, D), BF),
            pltpu.VMEM((slots, lanes), BF),
            pltpu.VMEM((slots, lanes), F32),
            pltpu.VMEM((D, D), BF),
            pltpu.VMEM((D, FF), BF),
            pltpu.VMEM((FF, D), BF),
            pltpu.VMEM((slots, D), BF),
            pltpu.VMEM((slots, 1), F32),
            pltpu.VMEM((slots, D), BF),
            pltpu.VMEM((slots, D), BF),
            pltpu.VMEM((slots, D), F32),
            pltpu.VMEM((BLK, D), F32),
            pltpu.VMEM((BLK, CHUNK), F32),
            pltpu.VMEM((BLK, CHUNK), F32),
            pltpu.VMEM((1, FF), F32),
            pltpu.VMEM((lanes, D), BF),
            pltpu.VMEM((D, lanes), BF),
            pltpu.VMEM((lanes, D), F32),
            pltpu.VMEM((lanes, D), F32),
            pltpu.SemaphoreType.DMA((3,)),
        ],
        compiler_params=params(60),
        cost_estimate=cost(50e9, 40 * 2**20),
        name="forward",
    )(
        rep_place, bucket, seg_lens, mixed, mixed, mixed, x, cot, mixed, *vectors,
        out_weight, fc_weight, proj_weight, *prefix_pieces,
    )

    copies = jnp.broadcast_to(prefix_row, (lax.axis_size("batch"), *prefix_row.shape))
    batch_rows = lax.all_to_all(copies, "batch", split_axis=0, concat_axis=0, tiled=True)

    pairs = HEADS // 2

    def pair_at(offset):
        return pl.BlockSpec((slots, 128), lambda g: (0, offset + g))

    stat_spec = pl.BlockSpec((2 * PAD, slots), lambda g: (g, 0))
    d_mixed = pl.pallas_call(
        attend_back_kernel,
        grid=(pairs,),
        out_shape=shape((3, slots, D), BF),
        in_specs=[
            SMEM,
            pair_at(0), pair_at(pairs), pair_at(2 * pairs), pair_at(0),
            pl.BlockSpec((PAD, 128), lambda g: (0, g)),
            pl.BlockSpec((slots, 128), lambda g: (0, g // 4)),
            stat_spec, stat_spec,
        ],
        out_specs=pl.BlockSpec((3, slots, 128), lambda g: (0, 0, g)),
        compiler_params=params(60),
        cost_estimate=cost(28e9, 20 * 2**20),
        name="attend_back",
    )(bucket, mixed, mixed, mixed, d_att, prefix_kv, d_sp, lse_t, delta_t)

    group_sum = jnp.sum(batch_rows.astype(F32), axis=0).astype(BF)
    rep_pieces = to_all(group_sum, "rep")

    tokens_grad = pl.pallas_call(
        project_back_kernel,
        grid=(3,),
        out_shape=shape((slots, D), BF),
        in_specs=[
            pl.BlockSpec((1, slots, D), lambda t: (t, 0, 0)),
            pl.BlockSpec((D, D), lambda t: (0, t)),
            whole(ln1_gain), ANY, ANY,
        ],
        out_specs=pl.BlockSpec((slots, D), lambda t: (0, 0)),
        scratch_shapes=[
            pltpu.VMEM((slots, D), F32),
            pltpu.VMEM((slots, D), BF),
            pltpu.VMEM((slots, D), F32),
            pltpu.SemaphoreType.DMA((2,)),
        ],
        compiler_params=params(60),
        cost_estimate=cost(6 * slots * D * D, 20 * 2**20),
        name="project_back",
    )(d_mixed, qkv_weight, ln1_gain, x, d_mid)

    tail_args = (tanh_pre, prefix_embed, reparam_in, *weight_pieces, *rep_pieces)
    tail_outs = (
        shape((PREFIX, D), F32),
        shape((D, hidden_width), F32),
        shape((1, hidden_width), F32),
        shape((hidden_width, own_width), F32),
        shape((1, own_width), F32),
    )
    embed_grad, in_grad, in_bias_grad, out_grad, out_bias_grad = pl.pallas_call(
        tail_kernel,
        grid=(1,),
        out_shape=tail_outs,
        in_specs=[SMEM] + [whole(arg) for arg in tail_args],
        out_specs=tuple(whole(out) for out in tail_outs),
        scratch_shapes=[
            pltpu.VMEM((PAD, D), F32),
            pltpu.VMEM((len(rep_pieces), *prefix_shape.shape), BF),
            pltpu.VMEM(prefix_shape.shape, BF),
            pltpu.VMEM((len(rep_pieces), PAD, hidden_width), F32),
        ],
        compiler_params=params(16),
        name="tail",
    )(rep_place, *tail_args)
    return (
        block_out[None],
        tokens_grad[None],
        embed_grad,
        in_grad,
        in_bias_grad[0],
        out_grad,
        out_bias_grad[0],
    )


def solution(mesh):
    row = P(("batch", "rep"), None, None)
    placed = (row, *[P()] * 15, P(None, "rep"), P("rep"), P(("batch", "rep")), P(("batch", "rep"), None), row)
    return jax.shard_map(
        local,
        mesh=mesh,
        in_specs=placed,
        out_specs=(row, row, P(), P(), P(), P(None, "rep"), P("rep")),
        check_vma=False,
    )
```

profile of v0, /device:TPU:0, one launch (start us, length us, event | category | flops | bytes accessed | tf_op | source)
XLA Modules:
  0.0 164.5 jit_solution(11400102409150396419)
XLA Ops:
  0.6 2.4 %reparam.1 = (f32[16,512]{1,0:T(8,128)}, bf16[16,512]{1,0:T(8,128)(2,1)}) custom-call(bf16[10,1024]{1,0:T(8,128)(2,1)} %embed_ref.3, bf16[1024,512]{1,0:T(8,128)(2,1)} %in_w_ref.3, bf16[512]{0:T(512)(128)(2,1)} %in_b_ref.1, bf16[512,512]{1,0:T(8,128)(2,1)} %refs_0_, bf16[512]{0:T(512)(128)(2,1)} %out_b_ref.2), custom_call_target="tpu_custom_call" | custom-call | tf_op jit(solution)/shard_map/reparam/pallas_call | solution.py:510
  3.0 0.5 collective-permute-start
  3.5 2.5 %collective-permute-start.1 = (bf16[16,512]{1,0:T(8,128)(2,1)}, bf16[16,512]{1,0:T(8,128)(2,1)S(1)}, u32[]{:S(2)}, u32[]{:S(2)}) collective-permute-start(bf16[16,512]{1,0:T(8,128)(2,1)} %get-tuple-element.23.refs_0_), channel_id=1, source_target_pairs={{0,2},{1,3},{2,0},{3,1},{4,6},{5,7},{6,4},{7,5},{8,10},{9,11},{10,... | collective-permute-start | bytes 49160 | tf_op jit(solution)/shard_map/ppermute | solution.py:491
  6.0 1.4 collective-permute-start.2
  7.4 0.0 copy-start.1
  7.4 11.7 %project.1.q_ref.k_ref.v_ref.q_rows_ref.refs_0_.refs_1_ = bf16[1024,3072]{1,0:T(8,128)(2,1)} custom-call(bf16[1024,1024]{1,0:T(8,128)(2,1)} %bitcast.8, bf16[1024]{0:T(1024)(128)(2,1)} %gain_ref.5, bf16[1024]{0:T(1024)(128)(2,1)} %shift_ref.2, bf16[3072]{0:T(1024)(128)(2,1)} %bias_ref.1, bf16[1024,3072]{1,0:T(8,128)(2,1)} %w_ref.3), custom_call_target="tpu_custom_call" | custom-call | flops 6442450944 | bytes 16777216 | tf_op jit(solution)/shard_map/project/pallas_call | solution.py:522
  19.1 0.0 copy-done.1
  19.1 0.0 collective-permute-start.3
  19.1 0.4 collective-permute-start.4
  20.2 0.0 collective-permute-done.refs_1_
  20.2 0.0 copy-start.4
  20.2 1.4 collective-permute-start.5
  21.6 0.0 collective-permute-done.1.refs_2_
  21.6 0.0 copy-start.5
  21.7 0.0 collective-permute-done.2.refs_3_
  21.7 0.0 copy-start.6
  21.7 0.0 copy-done.4
  21.7 0.6 copy-done.5
  22.2 0.0 copy-done.6
  22.3 84.7 %forward.1 = (bf16[1024,1024]{1,0:T(8,128)(2,1)}, f32[1024,1024]{1,0:T(8,128)}, bf16[1024,1024]{1,0:T(8,128)(2,1)}, bf16[1024,256]{1,0:T(8,128)(2,1)}, f32[256,1...) custom-call(s32[1]{0:T(128)} %bitcast.place_ref, ...), custom_call_target="tpu_custom_call" | custom-call | flops 49999998976 | bytes 41943040 | tf_op jit(solution)/shard_map/forward/pallas_call | solution.py:551
  106.9 1.7 %broadcast_in_dim.15 = bf16[8,16,2048]{2,1,0:T(8,128)(2,1)} broadcast(bf16[16,2048]{1,0:T(8,128)(2,1)} %get-tuple-element.33), dimensions={1,2} | broadcast | bytes 589824 | tf_op jit(solution)/shard_map/broadcast_in_dim | solution.py:603
  108.6 5.0 %all-to-all-start = ((bf16[8,16,2048]{2,1,0:T(8,128)(2,1)}), bf16[8,16,2048]{2,1,0:T(8,128)(2,1)S(1)}, u32[]{:S(2)}, u32[]{:S(2)}) async-start(bf16[8,16,2048]{2,1,0:T(8,128)(2,1)} %broadcast_in_dim.15), calls=%async_computation | async-start | bytes 1048576 | tf_op jit(solution)/shard_map/all_to_all | solution.py:604
  113.7 32.3 %attend_back.1.d_mix_ref = bf16[3,1024,1024]{2,1,0:T(8,128)(2,1)} custom-call(s32[1]{0:T(128)S(6)} %copy.28.bucket_ref, bf16[1024,3072]{1,0:T(8,128)(2,1)} %project.1.q_ref.k_ref.v_ref.q_rows_ref.refs_0_.refs_1_, bf16[1024,3072]{1,0:T(8,128)(2,1)} %project.1.q_ref.k_ref.v_ref.q_rows_ref.refs_0_.refs_1_, ...), custom_call_target="tpu_custom_call" | custom-call | flops 28000000000 | bytes 20971520 | tf_op jit(solution)/shard_map/attend_back/pallas_call | solution.py:612
  146.0 0.0 all-to-all-done
  146.0 0.1 reduce_sum.12.refs_4_
  146.1 0.1 collective-permute-start.6
  146.2 1.5 collective-permute-start.7
  147.7 0.0 collective-permute-done.3.refs_1_
  147.7 1.4 collective-permute-start.8
  149.1 0.0 copy-start
  149.1 0.0 copy-start.2
  149.1 0.0 copy-start.3
  149.1 12.8 %project_back.1 = bf16[1024,1024]{1,0:T(8,128)(2,1)} custom-call(bf16[3,1024,1024]{2,1,0:T(8,128)(2,1)} %attend_back.1.d_mix_ref, bf16[1024,3072]{1,0:T(8,128)(2,1)} %w_ref.3, bf16[1024]{0:T(1024)(128)(2,1)} %gain_ref.5, bf16[1024,1024]{1,0:T(8,128)(2,1)} %bitcast.10, f32[1024,1024]{1,0:T(8,128)} %get-tuple-element.30.d_mid_hbm), custom_call_target="tpu_custom_call" | custom-call | flops 6442450944 | bytes 20971520 | tf_op jit(solution)/shard_map/project_back/pallas_call | solution.py:632
  161.9 0.0 collective-permute-done.4.refs_2_
  161.9 0.0 collective-permute-done.5.refs_3_
  161.9 0.0 collective-permute-done.6.refs_5_
  161.9 0.0 collective-permute-done.7.refs_6_
  161.9 0.0 collective-permute-done.8.refs_7_
  161.9 0.0 copy-done
  161.9 0.0 copy-done.2
  162.0 0.0 copy-done.3
  162.0 2.6 %tail.1 = (f32[10,1024]{1,0:T(8,128)}, f32[1024,512]{1,0:T(8,128)}, f32[1,512]{1,0:T(1,128)}, f32[512,512]{1,0:T(8,128)}, f32[1,512]{1,0:T(1,128)}) custom-call(s32[1]{0:T(128)} %bitcast.place_ref, f32[16,512]{1,0:T(8,128)S(1)} %copy-done.3, bf16[10,1024]{1,0:T(8,128)(2,1)S(1)} %copy-done.2, bf16[1024,512]{1,0:T(8,128)(2,1)S(1)} %copy-done, ...), custom_call_target="tpu_custom_call" | custom-call | tf_op jit(solution)/shard_map/tail/pallas_call | solution.py:661
Async XLA Ops:
  3.0 17.2 %collective-permute-start = (bf16[16,512]{1,0:T(8,128)(2,1)}, bf16[16,512]{1,0:T(8,128)(2,1)S(1)}, u32[]{:S(2)}, u32[]{:S(2)}) collective-permute-start(bf16[16,512]{1,0:T(8,128)(2,1)} %get-tuple-element.23.refs_0_), channel_id=1, source_target_pairs={{0,1},{1,2},{2,3},{3,0},{4,5},{5,6},{6,7},{7,4},{8,9},{9,10},{10,1... | collective-permute-start | bytes 49160 | tf_op jit(solution)/shard_map/ppermute | solution.py:491
  3.5 18.2 %collective-permute-start.1 = (bf16[16,512]{1,0:T(8,128)(2,1)}, bf16[16,512]{1,0:T(8,128)(2,1)S(1)}, u32[]{:S(2)}, u32[]{:S(2)}) collective-permute-start(bf16[16,512]{1,0:T(8,128)(2,1)} %get-tuple-element.23.refs_0_), channel_id=1, source_target_pairs={{0,2},{1,3},{2,0},{3,1},{4,6},{5,7},{6,4},{7,5},{8,10},{9,11},{10,... | collective-permute-start | bytes 49160 | tf_op jit(solution)/shard_map/ppermute | solution.py:491
  6.0 15.6 %collective-permute-start.2 = (bf16[16,512]{1,0:T(8,128)(2,1)}, bf16[16,512]{1,0:T(8,128)(2,1)S(1)}, u32[]{:S(2)}, u32[]{:S(2)}) collective-permute-start(bf16[16,512]{1,0:T(8,128)(2,1)} %get-tuple-element.23.refs_0_), channel_id=1, source_target_pairs={{0,3},{1,0},{2,1},{3,2},{4,7},{5,4},{6,5},{7,6},{8,11},{9,8},{10,9... | collective-permute-start | bytes 49160 | tf_op jit(solution)/shard_map/ppermute | solution.py:491
  7.4 11.7 %copy-start.1 = (bf16[512,512]{1,0:T(8,128)(2,1)S(1)}, bf16[512,512]{1,0:T(8,128)(2,1)}, u32[]{:S(2)}) copy-start(bf16[512,512]{1,0:T(8,128)(2,1)} %refs_0_) | copy-start | bytes 1572868
  19.1 128.5 %collective-permute-start.3 = (bf16[512,512]{1,0:T(8,128)(2,1)S(1)}, bf16[512,512]{1,0:T(8,128)(2,1)S(1)}, u32[]{:S(2)}, u32[]{:S(2)}) collective-permute-start(bf16[512,512]{1,0:T(8,128)(2,1)S(1)} %copy-done.1), channel_id=1, source_target_pairs={{0,1},{1,2},{2,3},{3,0},{4,5},{5,6},{6,7},{7,4},{8,9},{9,10},{10,1... | collective-permute-start | bytes 1572872 | tf_op jit(solution)/shard_map/ppermute | solution.py:491
  19.1 142.7 %collective-permute-start.4 = (bf16[512,512]{1,0:T(8,128)(2,1)S(1)}, bf16[512,512]{1,0:T(8,128)(2,1)S(1)}, u32[]{:S(2)}, u32[]{:S(2)}) collective-permute-start(bf16[512,512]{1,0:T(8,128)(2,1)S(1)} %copy-done.1), channel_id=1, source_target_pairs={{0,2},{1,3},{2,0},{3,1},{4,6},{5,7},{6,4},{7,5},{8,10},{9,11},{10,... | collective-permute-start | bytes 1572872 | tf_op jit(solution)/shard_map/ppermute | solution.py:491
  20.2 1.5 copy-start.4
  20.2 141.7 %collective-permute-start.5 = (bf16[512,512]{1,0:T(8,128)(2,1)S(1)}, bf16[512,512]{1,0:T(8,128)(2,1)S(1)}, u32[]{:S(2)}, u32[]{:S(2)}) collective-permute-start(bf16[512,512]{1,0:T(8,128)(2,1)S(1)} %copy-done.1), channel_id=1, source_target_pairs={{0,3},{1,0},{2,1},{3,2},{4,7},{5,4},{6,5},{7,6},{8,11},{9,8},{10,9... | collective-permute-start | bytes 1572872 | tf_op jit(solution)/shard_map/ppermute | solution.py:491
  21.6 0.6 copy-start.5
  21.7 0.6 copy-start.6
  108.6 37.4 %all-to-all-start = ((bf16[8,16,2048]{2,1,0:T(8,128)(2,1)}), bf16[8,16,2048]{2,1,0:T(8,128)(2,1)S(1)}, u32[]{:S(2)}, u32[]{:S(2)}) async-start(bf16[8,16,2048]{2,1,0:T(8,128)(2,1)} %broadcast_in_dim.15), calls=%async_computation | async-start | bytes 1048576 | tf_op jit(solution)/shard_map/all_to_all | solution.py:604
  146.1 15.8 %collective-permute-start.6 = (bf16[16,2048]{1,0:T(8,128)(2,1)S(1)}, bf16[16,2048]{1,0:T(8,128)(2,1)S(1)}, u32[]{:S(2)}, u32[]{:S(2)}) collective-permute-start(bf16[16,2048]{1,0:T(8,128)(2,1)S(1)} %reduce_sum.12.refs_4_), channel_id=1, source_target_pairs={{0,1},{1,2},{2,3},{3,0},{4,5},{5,6},{6,7},{7,4},{8,9},{9,10},{10,1... | collective-permute-start | bytes 196616 | tf_op jit(solution)/shard_map/ppermute | solution.py:491
  146.2 15.8 %collective-permute-start.7 = (bf16[16,2048]{1,0:T(8,128)(2,1)S(1)}, bf16[16,2048]{1,0:T(8,128)(2,1)S(1)}, u32[]{:S(2)}, u32[]{:S(2)}) collective-permute-start(bf16[16,2048]{1,0:T(8,128)(2,1)S(1)} %reduce_sum.12.refs_4_), channel_id=1, source_target_pairs={{0,2},{1,3},{2,0},{3,1},{4,6},{5,7},{6,4},{7,5},{8,10},{9,11},{10,... | collective-permute-start | bytes 196616 | tf_op jit(solution)/shard_map/ppermute | solution.py:491
  147.7 14.3 %collective-permute-start.8 = (bf16[16,2048]{1,0:T(8,128)(2,1)S(1)}, bf16[16,2048]{1,0:T(8,128)(2,1)S(1)}, u32[]{:S(2)}, u32[]{:S(2)}) collective-permute-start(bf16[16,2048]{1,0:T(8,128)(2,1)S(1)} %reduce_sum.12.refs_4_), channel_id=1, source_target_pairs={{0,3},{1,0},{2,1},{3,2},{4,7},{5,4},{6,5},{7,6},{8,11},{9,8},{10,9... | collective-permute-start | bytes 196616 | tf_op jit(solution)/shard_map/ppermute | solution.py:491
  149.1 12.9 %copy-start = (bf16[1024,512]{1,0:T(8,128)(2,1)S(1)}, bf16[1024,512]{1,0:T(8,128)(2,1)}, u32[]{:S(2)}) copy-start(bf16[1024,512]{1,0:T(8,128)(2,1)} %in_w_ref.3) | copy-start | bytes 3145732
  149.1 12.9 %copy-start.2 = (bf16[10,1024]{1,0:T(8,128)(2,1)S(1)}, bf16[10,1024]{1,0:T(8,128)(2,1)}, u32[]{:S(2)}) copy-start(bf16[10,1024]{1,0:T(8,128)(2,1)} %embed_ref.3) | copy-start | bytes 61444
  149.1 12.9 %copy-start.3 = (f32[16,512]{1,0:T(8,128)S(1)}, f32[16,512]{1,0:T(8,128)}, u32[]{:S(2)}) copy-start(f32[16,512]{1,0:T(8,128)} %get-tuple-element.31.tanh_ref) | copy-start | bytes 98308
where the time goes:
time: 165 us
  Pallas kernels  146 us (88%)
  starting transfers between devices  14.3 us (9%)
  local copies, waits for them, and re-layouts  2.31 us (1%)
    pallas_call x1, Pallas kernels, local(): pl.pallas_call(forward_kernel, grid=(QUADS + 2 * blocks,), out_shape=(sha...  84.7 us
    pallas_call x1, Pallas kernels, local(): pl.pallas_call(attend_back_kernel, grid=(pairs,), out_shape=shape((3, slo...  32.3 us
    pallas_call x1, Pallas kernels, local(): pl.pallas_call(project_back_kernel, grid=(3,), out_shape=shape((slots, D)...  12.8 us
    pallas_call x1, Pallas kernels, local(): pl.pallas_call(project_kernel, grid=(3,), out_shape=shape((slots, 3 * D),...  11.7 us
    ppermute x9, starting transfers between devices, to_all(): lax.ppermute(value, axis, [(place, (place + shift) % size) for place in r...  9.22 us
    all_to_all x1, starting transfers between devices, local(): lax.all_to_all(copies, 'batch', split_axis=0, concat_axis=0, tiled=True)  5.04 us
  transfers between devices with their start and end apart: 10, of which 0 were waited for; matrix products, arithmetic and copies ran while one was open for 1% of the time, Pallas kernels for 86%

commit v1 on v0

--- a/solution.py
+++ b/solution.py
@@ -15,6 +15,7 @@
 BLK = 256
 QUAD = 4 * HEAD_DIM
 QUADS = HEADS // 4
+EARLY_PAIRS = 4
 CHUNK = 1024
 
 BF = jnp.bfloat16
@@ -104,9 +105,10 @@
         norm, _ = normalise(x_ref[first : first + BLK, :].astype(F32))
         normed_ref[first : first + BLK, :] = (norm * row_of(gain_ref) + row_of(shift_ref)).astype(BF)
 
-    def dot_part(first, rows):
-        mixed = dot_nn(normed_ref[first : first + rows, :], w_ref[...]) + row_of(bias_ref)
-        out_ref[first : first + rows, :] = (mixed.astype(BF).astype(F32) * factor).astype(BF)
+    def dot_part(first, count):
+        rows = pl.ds(first, count)
+        mixed = dot_nn(normed_ref[rows, :], w_ref[...]) + row_of(bias_ref)
+        out_ref[rows, :] = (mixed.astype(BF).astype(F32) * factor).astype(BF)
 
     @pl.when(step == 0)
     def _():
@@ -118,8 +120,11 @@
 
     @pl.when(step > 0)
     def _():
-        for first in range(0, slots, 2 * BLK):
-            dot_part(first, 2 * BLK)
+        def body(index, carry):
+            dot_part(pl.multiple_of(index * 2 * BLK, 2 * BLK), 2 * BLK)
+            return carry
+
+        lax.fori_loop(0, slots // (2 * BLK), body, 0)
 
 
 def live_column(bucket_ref, lens_ref, first, rows, slots):
@@ -133,9 +138,15 @@
     return position < jnp.where(bucket_ref[0] == slots, total, segment * SHORT + short_len)
 
 
-def attend(q_ref, k_ref, v_ref, prefix_ref, att_ref, pp_ref, lse_ref, quad, long_row):
-    slots = q_ref.shape[0]
-    blocks = slots // BLK
+def block_rows(block):
+    return pl.ds(block * BLK if isinstance(block, int) else pl.multiple_of(block * BLK, BLK), BLK)
+
+
+def key_rows(block, long_row):
+    return pl.ds(0, (block + 1) * BLK) if long_row else block_rows(block)
+
+
+def attend(q_ref, k_ref, v_ref, prefix_ref, att_ref, pp_ref, lse_ref, quad, query_blocks, long_row):
     cols = pl.ds(pl.multiple_of(quad * QUAD, QUAD), QUAD)
     pair_cols = pl.ds(pl.multiple_of((quad // 2) * 128, 128), 128)
     prefix_keys = quad_prefix(prefix_ref[:, cols], quad)
@@ -145,32 +156,28 @@
     lane_head = lane // PAD - 4 * (quad % 2)
     lane_real = lane % PAD < PREFIX
 
-    def keys_of(block):
-        return (0 if long_row else block * BLK), (block + 1) * BLK
-
     def scores(block, head):
-        first, last = keys_of(block)
         pair = slice(128 * (head // 2), 128 * (head // 2) + 128)
-        queries = q_ref[block * BLK : (block + 1) * BLK, pair]
+        queries = q_ref[block_rows(block), pair]
         queries = jnp.where(head_mask((BLK, 128), head), queries, jnp.zeros_like(queries))
-        raw = dot_nt(queries, k_ref[first:last, pair])
+        raw = dot_nt(queries, k_ref[key_rows(block, long_row), pair])
         own = jnp.where(causal, raw[:, -BLK:], masked_score)
-        return own if last - first == BLK else jnp.concatenate([raw[:, :-BLK], own], axis=1)
-
-    units = [(block, head) for block in range(blocks) for head in range(4)]
+        return own if raw.shape[1] == BLK else jnp.concatenate([raw[:, :-BLK], own], axis=1)
+
+    units = [(block, head) for block in query_blocks for head in range(4)]
     ahead = 2
     queue = [scores(*unit) for unit in units[:ahead]]
     for index, (block, head) in enumerate(units):
         if index + ahead < len(units):
             queue.append(scores(*units[index + ahead]))
-        rows = slice(block * BLK, (block + 1) * BLK)
+        rows = block_rows(block)
         if head == 0:
             prefix_raw = dot_nt(q_ref[rows, :], prefix_keys)
             probs_quad = jnp.zeros((BLK, 128), F32)
             lse_quad = jnp.zeros((BLK, 128), F32)
             outs = []
-        first, last = keys_of(block)
         pair = slice(128 * (head // 2), 128 * (head // 2) + 128)
+        count = queue[index].shape[1]
         prefix_scores = jnp.where((lane_head == head) & lane_real, prefix_raw, masked_score)
         score = jnp.concatenate([queue[index], prefix_scores], axis=1)
         queue[index] = None
@@ -178,8 +185,8 @@
         raised = jnp.exp(score - peak)
         summed = jnp.sum(raised, axis=1, keepdims=True)
         inv = 1.0 / summed
-        outs.append(dot_nn(raised[:, : last - first].astype(BF), v_ref[first:last, pair]) * inv)
-        probs_quad = probs_quad + raised[:, last - first :] * inv
+        outs.append(dot_nn(raised[:, :count].astype(BF), v_ref[key_rows(block, long_row), pair]) * inv)
+        probs_quad = probs_quad + raised[:, count:] * inv
         lse_quad = jnp.where(lane_head == head, peak + jnp.log(summed), lse_quad)
         if head == 3:
             probs_low = probs_quad.astype(BF)
@@ -204,11 +211,11 @@
     place_ref, bucket_ref, lens_ref, q_ref, k_ref, v_ref, x_ref, cot_ref, q_rows_ref,
     out_b_ref, gain_ref, shift_ref, fc_b_ref, proj_b_ref, out_w_hbm, fc_w_hbm, proj_w_hbm, *refs,
 ):
-    pieces, refs = refs[: len(refs) - 28], refs[len(refs) - 28 :]
+    pieces, refs = refs[: len(refs) - 29], refs[len(refs) - 29 :]
     (
-        block_ref, d_mid_ref, d_att_ref, d_sp_ref, lse_t_ref, delta_t_ref, prefix_row_ref, prefix_ref,
-        att_ref, pp_ref, lse_ref, out_w_ref, fc_w_ref, proj_w_ref, norm_ref, inv_ref, normed_ref, grad_out_ref,
-        acc_ref, d_acc_ref, pre_ref, d_act_ref, bias_ref, vp_ref, spread_ref, d_kp_ref, d_vp_ref, sems,
+        block_ref, d_mid_ref, d_att_ref, d_sp_ref, lse_t_ref, delta_t_ref, prefix_rows_hbm, prefix_ref,
+        att_ref, pp_ref, lse_ref, out_w_ref, fc_w_ref, proj_w_ref, norm_ref, normed_ref, grad_out_ref,
+        acc_ref, d_acc_ref, pre_ref, d_act_ref, bias_ref, vp_ref, spread_ref, d_kp_ref, d_vp_ref, row_ref, sems, row_sem,
     ) = refs
     step = pl.program_id(0)
     slots = q_ref.shape[0]
@@ -235,75 +242,68 @@
         d_kp_ref[...] = jnp.zeros_like(d_kp_ref)
         d_vp_ref[...] = jnp.zeros_like(d_vp_ref)
 
+    attend_args = (q_ref, k_ref, v_ref, prefix_ref, att_ref, pp_ref, lse_ref, step)
+
     @pl.when((step < QUADS) & long_row)
     def _():
-        attend(q_ref, k_ref, v_ref, prefix_ref, att_ref, pp_ref, lse_ref, step, True)
+        attend(*attend_args, list(range(slots // BLK)), True)
 
     @pl.when((step < QUADS) & jnp.logical_not(long_row))
     def _():
-        attend(q_ref, k_ref, v_ref, prefix_ref, att_ref, pp_ref, lse_ref, step, False)
-
-    blocks = slots // BLK
-    chunks = FF // CHUNK
+        def body(block, carry):
+            attend(*attend_args, [block], False)
+            return carry
+
+        lax.fori_loop(0, slots // BLK, body, 0)
 
     @pl.when(step == QUADS)
     def _():
-        copies[0].wait()
-
-    @pl.when((step >= QUADS) & (step < QUADS + blocks))
+        for copy in copies:
+            copy.wait()
+
+    @pl.when(step >= QUADS)
     def _():
         first = pl.multiple_of((step - QUADS) * BLK, BLK)
         rows = pl.ds(first, BLK)
-        mid = x_ref[...].astype(F32) + dot_nn(att_ref[rows, :], out_w_ref[...]) + row_of(out_b_ref)
+        live = live_column(bucket_ref, lens_ref, first, BLK, slots)
+        attended = att_ref[rows, :]
+        mid = x_ref[...].astype(F32) + dot_nn(attended, out_w_ref[...]) + row_of(out_b_ref)
         norm, inv = normalise(mid)
-        norm_ref[rows, :] = norm.astype(BF)
-        inv_ref[rows, :] = inv
-        normed_ref[rows, :] = (norm * row_of(gain_ref) + row_of(shift_ref)).astype(BF)
-        live = live_column(bucket_ref, lens_ref, first, BLK, slots)
-        grad_out_ref[rows, :] = jnp.where(live, cot_ref[...].astype(F32), 0.0).astype(BF)
-        acc_ref[rows, :] = mid + row_of(proj_b_ref)
-
-    def opened(block, chunk):
-        rows = pl.ds(pl.multiple_of(block * BLK, BLK), BLK)
-        part = pl.ds(pl.multiple_of(chunk * CHUNK, CHUNK), CHUNK)
-        pre = dot_nn(normed_ref[rows, :], fc_w_ref[:, part]) + bias_ref[:, part]
-        return pre, dot_nt(grad_out_ref[rows, :], proj_w_ref[part, :])
-
-    @pl.when(step == QUADS + blocks)
-    def _():
-        copies[1].wait()
-        copies[2].wait()
-        pre_ref[...], d_act_ref[...] = opened(jnp.int32(0), jnp.int32(0))
-
-    @pl.when(step >= QUADS + blocks)
-    def _():
-        block = step - QUADS - blocks
-        rows = pl.ds(pl.multiple_of(block * BLK, BLK), BLK)
+        norm_ref[...] = norm
+        normed_ref[...] = (norm * row_of(gain_ref) + row_of(shift_ref)).astype(BF)
+        grad_out_ref[...] = jnp.where(live, cot_ref[...].astype(F32), 0.0).astype(BF)
+        acc_ref[...] = mid + row_of(proj_b_ref)
         d_acc_ref[...] = jnp.zeros_like(d_acc_ref)
+
+        def opened(chunk):
+            part = pl.ds(pl.multiple_of(chunk * CHUNK, CHUNK), CHUNK)
+            pre = dot_nn(normed_ref[...], fc_w_ref[:, part]) + bias_ref[:, part]
+            return pre, dot_nt(grad_out_ref[...], proj_w_ref[part, :])
+
+        def closed(chunk, pre, d_act):
+            part = pl.ds(pl.multiple_of(chunk * CHUNK, CHUNK), CHUNK)
+            act, slope = gelu_pair(pre)
+            forth = dot_nn(act.astype(BF), proj_w_ref[part, :])
+            back = dot_nt((d_act * slope).astype(BF), fc_w_ref[:, part])
+            return acc_ref[...] + forth, d_acc_ref[...] + back
 
         def chunk_step(chunk, carry):
             pre, d_act = pre_ref[...], d_act_ref[...]
-            wraps = chunk == chunks - 1
-            following = opened(
-                jnp.where(wraps, jnp.minimum(block + 1, blocks - 1), block), jnp.where(wraps, 0, chunk + 1)
-            )
-            part = pl.ds(pl.multiple_of(chunk * CHUNK, CHUNK), CHUNK)
-            act, slope = gelu_pair(pre)
-            acc_ref[rows, :] += dot_nn(act.astype(BF), proj_w_ref[part, :])
-            d_acc_ref[...] += dot_nt((d_act * slope).astype(BF), fc_w_ref[:, part])
-            pre_ref[...], d_act_ref[...] = following
+            next_pre, next_d_act = opened(chunk + 1)
+            acc_ref[...], d_acc_ref[...] = closed(chunk, pre, d_act)
+            pre_ref[...], d_act_ref[...] = next_pre, next_d_act
             return carry
 
-        lax.fori_loop(0, chunks, chunk_step, 0)
-        live = live_column(bucket_ref, lens_ref, block * BLK, BLK, slots)
-        block_ref[...] = jnp.where(live, acc_ref[rows, :], 0.0).astype(BF)
-        d_mid = grad_out_ref[rows, :].astype(F32) + norm_back(
-            d_acc_ref[...] * row_of(gain_ref), norm_ref[rows, :].astype(F32), inv_ref[rows, :]
-        )
+        chunks = FF // CHUNK
+        pre_ref[...], d_act_ref[...] = opened(0)
+        lax.fori_loop(0, chunks - 1, chunk_step, 0)
+        result, d_normed = closed(chunks - 1, pre_ref[...], d_act_ref[...])
+        block_ref[...] = jnp.where(live, result, 0.0).astype(BF)
+        d_mid = grad_out_ref[...].astype(F32) + norm_back(d_normed * row_of(gain_ref), norm_ref[...], inv)
         d_mid_ref[...] = d_mid
         d_att = dot_nt(d_mid.astype(BF), out_w_ref[...]).astype(BF)
         d_att_ref[...] = d_att
-        product = (d_att.astype(F32) * att_ref[rows, :].astype(F32)).astype(BF)
+        product = (d_att.astype(F32) * attended.astype(F32)).astype(BF)
         delta = dot_nn(product, spread_ref[...])
         probs = pp_ref[rows, :]
         d_sp = (probs.astype(F32) * (dot_nt(d_att, vp_ref[...]) - delta)).astype(BF)
@@ -325,14 +325,20 @@
             total = kept[0:PAD, :]
             for head in range(1, HEADS):
                 total = total + kept[head * PAD : (head + 1) * PAD, :]
-            prefix_row_ref[:, index * D : (index + 1) * D] = total.astype(BF)
+            row_ref[:, index * D : (index + 1) * D] = total.astype(BF)
+        sends = [
+            pltpu.make_async_copy(row_ref, prefix_rows_hbm.at[place], row_sem)
+            for place in range(prefix_rows_hbm.shape[0])
+        ]
+        for send in sends:
+            send.start()
+        for send in sends:
+            send.wait()
 
 
 def attend_back(
-    q_ref, k_ref, v_ref, do_ref, pk_ref, dsp_ref, lse_ref, delta_ref, mix_ref, pair, long_row
+    q_ref, k_ref, v_ref, do_ref, pk_ref, dsp_ref, lse_ref, delta_ref, mix_ref, cols, pair, query_blocks, long_row
 ):
-    slots = q_ref.shape[0]
-    blocks = slots // BLK
     causal = lax.broadcasted_iota(jnp.int32, (BLK, BLK), 0) <= lax.broadcasted_iota(jnp.int32, (BLK, BLK), 1)
     left = head_mask((BLK, 128), 0)
     row = lax.broadcasted_iota(jnp.int32, (128, 128), 0) // PAD
@@ -340,94 +346,98 @@
     tiled = jnp.concatenate([pk_ref[...]] * 8, axis=0)
     prefix_keys = jnp.where(row == col + 2 * (pair % 4), tiled, jnp.zeros_like(tiled))
 
-    def keys_of(block):
-        return (0 if long_row else block * BLK), (block + 1) * BLK
-
     def opened(block, side):
-        first, last = keys_of(block)
-        rows = slice(block * BLK, (block + 1) * BLK)
+        rows, keys = block_rows(block), key_rows(block, long_row)
         mask = head_mask((BLK, 128), side)
         queries, d_out = q_ref[rows, :], do_ref[rows, :]
-        raw = dot_nt(k_ref[first:last, :], jnp.where(mask, queries, jnp.zeros_like(queries)))
-        d_prob = dot_nt(v_ref[first:last, :], jnp.where(mask, d_out, jnp.zeros_like(d_out)))
+        raw = dot_nt(k_ref[keys, :], jnp.where(mask, queries, jnp.zeros_like(queries)))
+        d_prob = dot_nt(v_ref[keys, :], jnp.where(mask, d_out, jnp.zeros_like(d_out)))
         own = jnp.where(causal, raw[-BLK:], masked_score)
-        return (own if last - first == BLK else jnp.concatenate([raw[:-BLK], own], axis=0)), d_prob
-
-    units = [(block, side) for block in range(blocks) for side in range(2)]
+        return (own if raw.shape[0] == BLK else jnp.concatenate([raw[:-BLK], own], axis=0)), d_prob
+
+    units = [(block, side) for block in query_blocks for side in range(2)]
     ahead = 2
     queue = [opened(*unit) for unit in units[:ahead]]
-    d_keys = [[None] * blocks for _ in range(2)]
-    d_vals = [[None] * blocks for _ in range(2)]
+    d_keys = [[None] * len(query_blocks) for _ in range(2)]
+    d_vals = [[None] * len(query_blocks) for _ in range(2)]
     d_queries = [None, None]
     for index, (block, side) in enumerate(units):
         if index + ahead < len(units):
             queue.append(opened(*units[index + ahead]))
         score, d_prob = queue[index]
         queue[index] = None
-        first, last = keys_of(block)
-        rows = slice(block * BLK, (block + 1) * BLK)
+        rows, keys = block_rows(block), key_rows(block, long_row)
         stat = slice(side * PAD, side * PAD + 1)
         prob = jnp.exp(score - lse_ref[stat, rows])
         d_score = (prob * (d_prob - delta_ref[stat, rows])).astype(BF)
-        d_queries[side] = dot_tn(d_score, k_ref[first:last, :])
+        d_queries[side] = dot_tn(d_score, k_ref[keys, :])
         d_key = dot_nn(d_score, q_ref[rows, :])
         d_val = dot_nn(prob.astype(BF), do_ref[rows, :])
-        for place, key_block in enumerate(range(first // BLK, last // BLK)):
+        for place in range(d_key.shape[0] // BLK):
             part = slice(place * BLK, (place + 1) * BLK)
             for sums, value in ((d_keys, d_key), (d_vals, d_val)):
-                so_far = sums[side][key_block]
-                sums[side][key_block] = value[part] if so_far is None else so_far + value[part]
+                so_far = sums[side][place]
+                sums[side][place] = value[part] if so_far is None else so_far + value[part]
         if side == 1:
             d_query = jnp.where(left, d_queries[0], d_queries[1]) + dot_nn(dsp_ref[rows, :], prefix_keys)
-            mix_ref[0, rows, :] = (d_query * HEAD_DIM**-0.5).astype(BF)
-    for block in range(blocks):
-        rows = slice(block * BLK, (block + 1) * BLK)
-        mix_ref[1, rows, :] = jnp.where(left, d_keys[0][block], d_keys[1][block]).astype(BF)
-        mix_ref[2, rows, :] = jnp.where(left, d_vals[0][block], d_vals[1][block]).astype(BF)
-
-
-def attend_back_kernel(bucket_ref, q_ref, *refs):
-    args = (q_ref, *refs, pl.program_id(0))
-    long_row = bucket_ref[0] == q_ref.shape[0]
-
-    @pl.when(long_row)
-    def _():
-        attend_back(*args, True)
-
-    @pl.when(jnp.logical_not(long_row))
-    def _():
-        attend_back(*args, False)
-
-
-def project_back_kernel(d_mix_ref, w_ref, gain_ref, x_hbm, d_mid_hbm, grad_ref, acc_ref, x_ref, d_mid_ref, sems):
+            mix_ref[0, rows, cols] = (d_query * HEAD_DIM**-0.5).astype(BF)
+    for place, block in enumerate(query_blocks):
+        rows = block_rows(block)
+        mix_ref[1, rows, cols] = jnp.where(left, d_keys[0][place], d_keys[1][place]).astype(BF)
+        mix_ref[2, rows, cols] = jnp.where(left, d_vals[0][place], d_vals[1][place]).astype(BF)
+
+
+def attend_back_pair(bucket_ref, refs, mix_ref, cols, pair, here):
+    blocks = refs[0].shape[0] // BLK
+    long_row = bucket_ref[0] == refs[0].shape[0]
+    args = (*refs, mix_ref, cols, pair)
+
+    @pl.when(here & long_row)
+    def _():
+        attend_back(*args, list(range(blocks)), True)
+
+    @pl.when(here & jnp.logical_not(long_row))
+    def _():
+        def body(block, carry):
+            attend_back(*args, [block], False)
+            return carry
+
+        lax.fori_loop(0, blocks, body, 0)
+
+
+def early_back_kernel(bucket_ref, *refs):
+    *refs, mix_ref = refs
     step = pl.program_id(0)
-    last = pl.num_programs(0) - 1
-    slots = x_ref.shape[0]
-    copies = [
-        pltpu.make_async_copy(x_hbm, x_ref, sems.at[0]),
-        pltpu.make_async_copy(d_mid_hbm, d_mid_ref, sems.at[1]),
-    ]
+    attend_back_pair(bucket_ref, refs, mix_ref, slice(0, 128), step, step >= 0)
+
+
+def backward_kernel(bucket_ref, *refs):
+    refs, (early_ref, x_ref, d_mid_ref, gain_ref, w_hbm, grad_ref, mix_ref, w_ref, sem) = refs[:8], refs[8:]
+    step = pl.program_id(0)
+    pairs = mix_ref.shape[2] // 128
+    copy = pltpu.make_async_copy(w_hbm, w_ref, sem)
 
     @pl.when(step == 0)
     def _():
-        for copy in copies:
-            copy.start()
-        acc_ref[...] = dot_nt(d_mix_ref[0], w_ref[...])
-
-    @pl.when((step > 0) & (step < last))
-    def _():
-        acc_ref[...] += dot_nt(d_mix_ref[0], w_ref[...])
-
-    @pl.when(step == last)
-    def _():
-        for copy in copies:
-            copy.wait()
-        for first in range(0, slots, BLK):
-            rows = slice(first, first + BLK)
-            d_normed = acc_ref[rows, :] + dot_nt(d_mix_ref[0, rows, :], w_ref[...])
-            norm, inv = normalise(x_ref[rows, :].astype(F32))
-            back = norm_back(d_normed * row_of(gain_ref), norm, inv)
-            grad_ref[rows, :] = (d_mid_ref[rows, :] + back).astype(BF)
+        copy.start()
+
+    cols = pl.ds(pl.multiple_of(jnp.minimum(step, pairs - 1) * 128, 128), 128)
+    attend_back_pair(bucket_ref, refs, mix_ref, cols, step + (HEADS // 2 - pairs), step < pairs)
+
+    @pl.when(step == pairs)
+    def _():
+        copy.wait()
+
+    @pl.when(step >= pairs)
+    def _():
+        rows = block_rows(step - pairs)
+        d_mixed = jnp.concatenate(
+            [part for third in range(3) for part in (early_ref[third], mix_ref[third, rows, :])], axis=1
+        )
+        d_normed = dot_nt(d_mixed, w_ref[...])
+        norm, inv = normalise(x_ref[...].astype(F32))
+        back = norm_back(d_normed * row_of(gain_ref), norm, inv)
+        grad_ref[...] = (d_mid_ref[...] + back).astype(BF)
 
 
 def summed_in_order(place, pieces, ordered_ref):
@@ -540,17 +550,16 @@
     def quad_at(offset):
         return pl.BlockSpec((slots, QUAD), lambda g: (0, offset + jnp.minimum(g, QUADS - 1)))
 
-    def block_of(width, start):
-        return pl.BlockSpec((BLK, width), lambda g: (jnp.clip(g - start, 0, blocks - 1), 0))
+    def block_of(width):
+        return pl.BlockSpec((BLK, width), lambda g: (jnp.maximum(g - QUADS, 0), 0))
 
     lanes = HEADS * PAD
-    late = QUADS + blocks
-    block_t = pl.BlockSpec((lanes, BLK), lambda g: (0, jnp.clip(g - late, 0, blocks - 1)))
+    block_t = pl.BlockSpec((lanes, BLK), lambda g: (0, jnp.maximum(g - QUADS, 0)))
     vectors = (out_bias, ln2_gain, ln2_shift, fc_bias, proj_bias)
     prefix_shape = shape((PAD, 2 * D), BF)
-    block_out, d_mid, d_att, d_sp, lse_t, delta_t, prefix_row, prefix_kv = pl.pallas_call(
+    block_out, d_mid, d_att, d_sp, lse_t, delta_t, prefix_rows, prefix_kv = pl.pallas_call(
         forward_kernel,
-        grid=(QUADS + 2 * blocks,),
+        grid=(QUADS + blocks,),
         out_shape=(
             shape((slots, D), BF),
             shape((slots, D), F32),
@@ -558,17 +567,17 @@
             shape((slots, lanes), BF),
             shape((lanes, slots), F32),
             shape((lanes, slots), F32),
-            prefix_shape,
+            shape((lax.axis_size("batch"), *prefix_shape.shape), BF),
             prefix_shape,
         ),
         in_specs=[
             SMEM, SMEM, SMEM, quad_at(0), quad_at(QUADS), quad_at(2 * QUADS),
-            block_of(D, QUADS), block_of(D, QUADS), block_of(D, late),
+            block_of(D), block_of(D), block_of(D),
             *[whole(vector) for vector in vectors], ANY, ANY, ANY, *[whole(piece) for piece in prefix_pieces],
         ],
         out_specs=(
-            block_of(D, late), block_of(D, late), block_of(D, late), block_of(lanes, late), block_t, block_t,
-            whole(prefix_shape), whole(prefix_shape),
+            block_of(D), block_of(D), block_of(D), block_of(lanes), block_t, block_t,
+            ANY, whole(prefix_shape),
         ),
         scratch_shapes=[
             pltpu.VMEM((slots, D), BF),
@@ -577,11 +586,10 @@
             pltpu.VMEM((D, D), BF),
             pltpu.VMEM((D, FF), BF),
             pltpu.VMEM((FF, D), BF),
-            pltpu.VMEM((slots, D), BF),
-            pltpu.VMEM((slots, 1), F32),
-            pltpu.VMEM((slots, D), BF),
-            pltpu.VMEM((slots, D), BF),
-            pltpu.VMEM((slots, D), F32),
+            pltpu.VMEM((BLK, D), F32),
+            pltpu.VMEM((BLK, D), BF),
+            pltpu.VMEM((BLK, D), BF),
+            pltpu.VMEM((BLK, D), F32),
             pltpu.VMEM((BLK, D), F32),
             pltpu.VMEM((BLK, CHUNK), F32),
             pltpu.VMEM((BLK, CHUNK), F32),
@@ -590,7 +598,9 @@
             pltpu.VMEM((D, lanes), BF),
             pltpu.VMEM((lanes, D), F32),
             pltpu.VMEM((lanes, D), F32),
+            pltpu.VMEM(prefix_shape.shape, BF),
             pltpu.SemaphoreType.DMA((3,)),
+            pltpu.SemaphoreType.DMA,
         ],
         compiler_params=params(60),
         cost_estimate=cost(50e9, 40 * 2**20),
@@ -600,55 +610,63 @@
         out_weight, fc_weight, proj_weight, *prefix_pieces,
     )
 
-    copies = jnp.broadcast_to(prefix_row, (lax.axis_size("batch"), *prefix_row.shape))
-    batch_rows = lax.all_to_all(copies, "batch", split_axis=0, concat_axis=0, tiled=True)
+    batch_rows = lax.all_to_all(prefix_rows, "batch", split_axis=0, concat_axis=0, tiled=True)
 
     pairs = HEADS // 2
-
-    def pair_at(offset):
-        return pl.BlockSpec((slots, 128), lambda g: (0, offset + g))
-
-    stat_spec = pl.BlockSpec((2 * PAD, slots), lambda g: (g, 0))
-    d_mixed = pl.pallas_call(
-        attend_back_kernel,
-        grid=(pairs,),
-        out_shape=shape((3, slots, D), BF),
-        in_specs=[
+    early = EARLY_PAIRS
+
+    def back_specs(start, count):
+        def pair_of(g):
+            return start + jnp.minimum(g, count - 1)
+
+        def pair_at(offset):
+            return pl.BlockSpec((slots, 128), lambda g: (0, offset + pair_of(g)))
+
+        stat_spec = pl.BlockSpec((2 * PAD, slots), lambda g: (pair_of(g), 0))
+        return [
             SMEM,
             pair_at(0), pair_at(pairs), pair_at(2 * pairs), pair_at(0),
-            pl.BlockSpec((PAD, 128), lambda g: (0, g)),
-            pl.BlockSpec((slots, 128), lambda g: (0, g // 4)),
+            pl.BlockSpec((PAD, 128), lambda g: (0, pair_of(g))),
+            pl.BlockSpec((slots, 128), lambda g: (0, pair_of(g) // 4)),
             stat_spec, stat_spec,
-        ],
+        ]
+
+    back_args = (bucket, mixed, mixed, mixed, d_att, prefix_kv, d_sp, lse_t, delta_t)
+    d_mixed = pl.pallas_call(
+        early_back_kernel,
+        grid=(early,),
+        out_shape=shape((3, slots, early * 128), BF),
+        in_specs=back_specs(0, early),
         out_specs=pl.BlockSpec((3, slots, 128), lambda g: (0, 0, g)),
         compiler_params=params(60),
-        cost_estimate=cost(28e9, 20 * 2**20),
-        name="attend_back",
-    )(bucket, mixed, mixed, mixed, d_att, prefix_kv, d_sp, lse_t, delta_t)
+        cost_estimate=cost(14e9, 10 * 2**20),
+        name="early_back",
+    )(*back_args)
 
     group_sum = jnp.sum(batch_rows.astype(F32), axis=0).astype(BF)
     rep_pieces = to_all(group_sum, "rep")
 
+    late = pairs - early
+    late_rows = pl.BlockSpec((BLK, D), lambda g: (jnp.maximum(g - late, 0), 0))
     tokens_grad = pl.pallas_call(
-        project_back_kernel,
-        grid=(3,),
+        backward_kernel,
+        grid=(late + blocks,),
         out_shape=shape((slots, D), BF),
         in_specs=[
-            pl.BlockSpec((1, slots, D), lambda t: (t, 0, 0)),
-            pl.BlockSpec((D, D), lambda t: (0, t)),
-            whole(ln1_gain), ANY, ANY,
+            *back_specs(early, late),
+            pl.BlockSpec((3, BLK, early * 128), lambda g: (0, jnp.maximum(g - late, 0), 0)),
+            late_rows, late_rows, whole(ln1_gain), ANY,
         ],
-        out_specs=pl.BlockSpec((slots, D), lambda t: (0, 0)),
+        out_specs=late_rows,
         scratch_shapes=[
-            pltpu.VMEM((slots, D), F32),
-            pltpu.VMEM((slots, D), BF),
-            pltpu.VMEM((slots, D), F32),
-            pltpu.SemaphoreType.DMA((2,)),
+            pltpu.VMEM((3, slots, late * 128), BF),
+            pltpu.VMEM((D, 3 * D), BF),
+            pltpu.SemaphoreType.DMA,
         ],
         compiler_params=params(60),
-        cost_estimate=cost(6 * slots * D * D, 20 * 2**20),
-        name="project_back",
-    )(d_mixed, qkv_weight, ln1_gain, x, d_mid)
+        cost_estimate=cost(24e9, 30 * 2**20),
+        name="backward",
+    )(*back_args, d_mixed, x, d_mid, ln1_gain, qkv_weight)
 
     tail_args = (tanh_pre, prefix_embed, reparam_in, *weight_pieces, *rep_pieces)
     tail_outs = (

time: 165 us -> 158 us (0.958)
  Pallas kernels: 146 us -> 142 us
  local copies, waits for them, and re-layouts: 2.31 us -> 0.61 us
    pallas_call x3, Pallas kernels: 130 us -> 125 us  [the longest x1 80.3 us: local(): pl.pallas_call(forward_kernel, grid=(QUADS + blocks,), out_shape=(shape((...]
    broadcast_in_dim x1 -> x0, local copies, waits for them, and re-layouts: 1.69 us -> none  [local(): jnp.broadcast_to(prefix_row, (lax.axis_size('batch'), *prefix_row.shape))]
  transfers between devices with their start and end apart: 10 -> 10, of which waited for: 0 -> 0; matrix products, arithmetic and copies ran while one was open for 1% -> 0% of each run, Pallas kernels for 86% -> 87%
where the time goes in v1:
time: 158 us; the launch traced here: 157 us
  Pallas kernels  142 us (90%)
  starting transfers between devices  13.1 us (8%)
    pallas_call x1, Pallas kernels, local(): pl.pallas_call(forward_kernel, grid=(QUADS + blocks,), out_shape=(shape((...  80.3 us
    pallas_call x1, Pallas kernels, local(): pl.pallas_call(backward_kernel, grid=(late + blocks,), out_shape=shape((s...  27.2 us
    pallas_call x1, Pallas kernels, local(): pl.pallas_call(early_back_kernel, grid=(early,), out_shape=shape((3, slot...  17.3 us
    pallas_call x1, Pallas kernels, local(): pl.pallas_call(project_kernel, grid=(3,), out_shape=shape((slots, 3 * D),...  12 us
    ppermute x9, starting transfers between devices, to_all(): lax.ppermute(value, axis, [(place, (place + shift) % size) for place in r...  8.08 us
    all_to_all x1, starting transfers between devices, local(): lax.all_to_all(prefix_rows, 'batch', split_axis=0, concat_axis=0, tiled=T...  4.98 us
  transfers between devices with their start and end apart: 10, of which 0 were waited for; matrix products, arithmetic and copies ran while one was open for 0% of the time, Pallas kernels for 87%

profile of v1, /device:TPU:0, one launch (start us, length us, event | category | flops | bytes accessed | tf_op | source)
XLA Modules:
  0.0 157.0 jit_solution(4203169359427487714)
XLA Ops:
  0.6 2.4 %reparam.1 = (f32[16,512]{1,0:T(8,128)}, bf16[16,512]{1,0:T(8,128)(2,1)}) custom-call(bf16[10,1024]{1,0:T(8,128)(2,1)} %embed_ref.3, bf16[1024,512]{1,0:T(8,128)(2,1)} %in_w_ref.3, bf16[512]{0:T(512)(128)(2,1)} %in_b_ref.1, bf16[512,512]{1,0:T(8,128)(2,1)} %refs_0_, bf16[512]{0:T(512)(128)(2,1)} %out_b_ref.2), custom_call_target="tpu_custom_call" | custom-call | tf_op jit(solution)/shard_map/reparam/pallas_call | solution.py:520
  3.0 0.5 collective-permute-start
  3.5 2.5 %collective-permute-start.1 = (bf16[16,512]{1,0:T(8,128)(2,1)}, bf16[16,512]{1,0:T(8,128)(2,1)S(1)}, u32[]{:S(2)}, u32[]{:S(2)}) collective-permute-start(bf16[16,512]{1,0:T(8,128)(2,1)} %get-tuple-element.23.refs_0_), channel_id=1, source_target_pairs={{0,2},{1,3},{2,0},{3,1},{4,6},{5,7},{6,4},{7,5},{8,10},{9,11},{10,... | collective-permute-start | bytes 49160 | tf_op jit(solution)/shard_map/ppermute | solution.py:501
  6.0 1.4 collective-permute-start.2
  7.4 0.0 copy-start.1
  7.4 12.0 %project.1.q_ref.k_ref.v_ref.q_rows_ref.refs_0_.refs_1_.refs_2_ = bf16[1024,3072]{1,0:T(8,128)(2,1)} custom-call(bf16[1024,1024]{1,0:T(8,128)(2,1)} %bitcast.8, bf16[1024]{0:T(1024)(128)(2,1)} %refs_11_.1, bf16[1024]{0:T(1024)(128)(2,1)} %shift_ref.2, bf16[3072]{0:T(1024)(128)(2,1)} %bias_ref.1, bf16[1024,3072]{1,0:T(8,128)(2,1)} %refs_12_.1), custom_call_target="tpu_custom_call" | custom-call | flops 6442450944 | bytes 16777216 | tf_op jit(solution)/shard_map/project/pallas_call | solution.py:532
  19.4 0.0 copy-done.1
  19.4 0.0 collective-permute-start.3
  19.4 0.4 collective-permute-start.4
  20.5 0.0 collective-permute-done.refs_1_
  20.5 0.0 copy-start.4
  20.5 1.4 collective-permute-start.5
  22.0 0.0 collective-permute-done.1.refs_2_
  22.0 0.0 copy-start.5
  22.0 0.0 collective-permute-done.2.refs_3_
  22.0 0.0 copy-start.6
  22.0 0.0 copy-done.4
  22.0 0.6 copy-done.5
  22.6 0.0 copy-done.6
  22.6 80.3 %forward.1 = (bf16[1024,1024]{1,0:T(8,128)(2,1)}, f32[1024,1024]{1,0:T(8,128)}, bf16[1024,1024]{1,0:T(8,128)(2,1)}, bf16[1024,256]{1,0:T(8,128)(2,1)}, f32[256,1...) custom-call(s32[1]{0:T(128)} %bitcast.place_ref, ...), custom_call_target="tpu_custom_call" | custom-call | flops 49999998976 | bytes 41943040 | tf_op jit(solution)/shard_map/forward/pallas_call | solution.py:560
  102.9 5.0 %all-to-all-start = ((bf16[8,16,2048]{2,1,0:T(8,128)(2,1)}), bf16[8,16,2048]{2,1,0:T(8,128)(2,1)S(1)}, u32[]{:S(2)}, u32[]{:S(2)}) async-start(bf16[8,16,2048]{2,1,0:T(8,128)(2,1)} %get-tuple-element.33), calls=%async_computation | async-start | bytes 1048576 | tf_op jit(solution)/shard_map/all_to_all | solution.py:613
  107.9 17.3 %early_back.1.refs_8_ = bf16[3,1024,512]{2,1,0:T(8,128)(2,1)} custom-call(s32[1]{0:T(128)S(6)} %copy.28.bucket_ref, bf16[1024,3072]{1,0:T(8,128)(2,1)} %project.1.q_ref.k_ref.v_ref.q_rows_ref.refs_0_.refs_1_.refs_2_, bf16[1024,3072]{1,0:T(8,128)(2,1)} %project.1.q_ref.k_ref.v_ref.q_rows_ref.refs_0_.refs_1_.refs_2_, ...), custom_call_target="tpu_custom_call" | custom-call | flops 14000000000 | bytes 10485760 | tf_op jit(solution)/shard_map/early_back/pallas_call | solution.py:635
  125.2 0.0 all-to-all-done
  125.2 0.1 reduce_sum.12.refs_4_
  125.3 0.1 collective-permute-start.6
  125.3 0.1 collective-permute-start.7
  125.4 0.0 collective-permute-done.3.refs_1_
  125.4 1.7 %collective-permute-start.8 = (bf16[16,2048]{1,0:T(8,128)(2,1)S(1)}, bf16[16,2048]{1,0:T(8,128)(2,1)S(1)}, u32[]{:S(2)}, u32[]{:S(2)}) collective-permute-start(bf16[16,2048]{1,0:T(8,128)(2,1)S(1)} %reduce_sum.12.refs_4_), channel_id=1, source_target_pairs={{0,3},{1,0},{2,1},{3,2},{4,7},{5,4},{6,5},{7,6},{8,11},{9,8},{10,9... | collective-permute-start | bytes 196616 | tf_op jit(solution)/shard_map/ppermute | solution.py:501
  127.1 0.0 copy-start
  127.1 0.0 copy-start.2
  127.1 0.0 copy-start.3
  127.1 27.2 %backward.1 = bf16[1024,1024]{1,0:T(8,128)(2,1)} custom-call(s32[1]{0:T(128)S(6)} %copy.28.bucket_ref, bf16[1024,3072]{1,0:T(8,128)(2,1)} %project.1.q_ref.k_ref.v_ref.q_rows_ref.refs_0_.refs_1_.refs_2_, bf16[1024,3072]{1,0:T(8,128)(2,1)} %project.1.q_ref.k_ref.v_ref.q_rows_ref.refs_0_.refs_1_.refs_2_, ...), custom_call_target="tpu_custom_call" | custom-call | flops 24000000000 | bytes 31457280 | tf_op jit(solution)/shard_map/backward/pallas_call | solution.py:651
  154.3 0.0 collective-permute-done.4.refs_2_
  154.3 0.0 collective-permute-done.5.refs_3_
  154.3 0.0 collective-permute-done.6.refs_5_
  154.4 0.0 collective-permute-done.7.refs_6_
  154.4 0.0 collective-permute-done.8.refs_7_
  154.4 0.0 copy-done
  154.4 0.0 copy-done.2
  154.4 0.0 copy-done.3
  154.4 2.6 %tail.1 = (f32[10,1024]{1,0:T(8,128)}, f32[1024,512]{1,0:T(8,128)}, f32[1,512]{1,0:T(1,128)}, f32[512,512]{1,0:T(8,128)}, f32[1,512]{1,0:T(1,128)}) custom-call(s32[1]{0:T(128)} %bitcast.place_ref, f32[16,512]{1,0:T(8,128)S(1)} %copy-done.3, bf16[10,1024]{1,0:T(8,128)(2,1)S(1)} %copy-done.2, bf16[1024,512]{1,0:T(8,128)(2,1)S(1)} %copy-done, ...), custom_call_target="tpu_custom_call" | custom-call | tf_op jit(solution)/shard_map/tail/pallas_call | solution.py:679
Async XLA Ops:
  3.0 17.5 %collective-permute-start = (bf16[16,512]{1,0:T(8,128)(2,1)}, bf16[16,512]{1,0:T(8,128)(2,1)S(1)}, u32[]{:S(2)}, u32[]{:S(2)}) collective-permute-start(bf16[16,512]{1,0:T(8,128)(2,1)} %get-tuple-element.23.refs_0_), channel_id=1, source_target_pairs={{0,1},{1,2},{2,3},{3,0},{4,5},{5,6},{6,7},{7,4},{8,9},{9,10},{10,1... | collective-permute-start | bytes 49160 | tf_op jit(solution)/shard_map/ppermute | solution.py:501
  3.5 18.5 %collective-permute-start.1 = (bf16[16,512]{1,0:T(8,128)(2,1)}, bf16[16,512]{1,0:T(8,128)(2,1)S(1)}, u32[]{:S(2)}, u32[]{:S(2)}) collective-permute-start(bf16[16,512]{1,0:T(8,128)(2,1)} %get-tuple-element.23.refs_0_), channel_id=1, source_target_pairs={{0,2},{1,3},{2,0},{3,1},{4,6},{5,7},{6,4},{7,5},{8,10},{9,11},{10,... | collective-permute-start | bytes 49160 | tf_op jit(solution)/shard_map/ppermute | solution.py:501
  6.0 16.0 %collective-permute-start.2 = (bf16[16,512]{1,0:T(8,128)(2,1)}, bf16[16,512]{1,0:T(8,128)(2,1)S(1)}, u32[]{:S(2)}, u32[]{:S(2)}) collective-permute-start(bf16[16,512]{1,0:T(8,128)(2,1)} %get-tuple-element.23.refs_0_), channel_id=1, source_target_pairs={{0,3},{1,0},{2,1},{3,2},{4,7},{5,4},{6,5},{7,6},{8,11},{9,8},{10,9... | collective-permute-start | bytes 49160 | tf_op jit(solution)/shard_map/ppermute | solution.py:501
  7.4 12.0 %copy-start.1 = (bf16[512,512]{1,0:T(8,128)(2,1)S(1)}, bf16[512,512]{1,0:T(8,128)(2,1)}, u32[]{:S(2)}) copy-start(bf16[512,512]{1,0:T(8,128)(2,1)} %refs_0_) | copy-start | bytes 1572868
  19.4 106.0 %collective-permute-start.3 = (bf16[512,512]{1,0:T(8,128)(2,1)S(1)}, bf16[512,512]{1,0:T(8,128)(2,1)S(1)}, u32[]{:S(2)}, u32[]{:S(2)}) collective-permute-start(bf16[512,512]{1,0:T(8,128)(2,1)S(1)} %copy-done.1), channel_id=1, source_target_pairs={{0,1},{1,2},{2,3},{3,0},{4,5},{5,6},{6,7},{7,4},{8,9},{9,10},{10,1... | collective-permute-start | bytes 1572872 | tf_op jit(solution)/shard_map/ppermute | solution.py:501
  19.4 134.9 %collective-permute-start.4 = (bf16[512,512]{1,0:T(8,128)(2,1)S(1)}, bf16[512,512]{1,0:T(8,128)(2,1)S(1)}, u32[]{:S(2)}, u32[]{:S(2)}) collective-permute-start(bf16[512,512]{1,0:T(8,128)(2,1)S(1)} %copy-done.1), channel_id=1, source_target_pairs={{0,2},{1,3},{2,0},{3,1},{4,6},{5,7},{6,4},{7,5},{8,10},{9,11},{10,... | collective-permute-start | bytes 1572872 | tf_op jit(solution)/shard_map/ppermute | solution.py:501
  20.5 1.5 copy-start.4
  20.5 133.8 %collective-permute-start.5 = (bf16[512,512]{1,0:T(8,128)(2,1)S(1)}, bf16[512,512]{1,0:T(8,128)(2,1)S(1)}, u32[]{:S(2)}, u32[]{:S(2)}) collective-permute-start(bf16[512,512]{1,0:T(8,128)(2,1)S(1)} %copy-done.1), channel_id=1, source_target_pairs={{0,3},{1,0},{2,1},{3,2},{4,7},{5,4},{6,5},{7,6},{8,11},{9,8},{10,9... | collective-permute-start | bytes 1572872 | tf_op jit(solution)/shard_map/ppermute | solution.py:501
  22.0 0.6 copy-start.5
  22.0 0.6 copy-start.6
  102.9 22.3 %all-to-all-start = ((bf16[8,16,2048]{2,1,0:T(8,128)(2,1)}), bf16[8,16,2048]{2,1,0:T(8,128)(2,1)S(1)}, u32[]{:S(2)}, u32[]{:S(2)}) async-start(bf16[8,16,2048]{2,1,0:T(8,128)(2,1)} %get-tuple-element.33), calls=%async_computation | async-start | bytes 1048576 | tf_op jit(solution)/shard_map/all_to_all | solution.py:613
  125.3 29.1 %collective-permute-start.6 = (bf16[16,2048]{1,0:T(8,128)(2,1)S(1)}, bf16[16,2048]{1,0:T(8,128)(2,1)S(1)}, u32[]{:S(2)}, u32[]{:S(2)}) collective-permute-start(bf16[16,2048]{1,0:T(8,128)(2,1)S(1)} %reduce_sum.12.refs_4_), channel_id=1, source_target_pairs={{0,1},{1,2},{2,3},{3,0},{4,5},{5,6},{6,7},{7,4},{8,9},{9,10},{10,1... | collective-permute-start | bytes 196616 | tf_op jit(solution)/shard_map/ppermute | solution.py:501
  125.3 29.0 %collective-permute-start.7 = (bf16[16,2048]{1,0:T(8,128)(2,1)S(1)}, bf16[16,2048]{1,0:T(8,128)(2,1)S(1)}, u32[]{:S(2)}, u32[]{:S(2)}) collective-permute-start(bf16[16,2048]{1,0:T(8,128)(2,1)S(1)} %reduce_sum.12.refs_4_), channel_id=1, source_target_pairs={{0,2},{1,3},{2,0},{3,1},{4,6},{5,7},{6,4},{7,5},{8,10},{9,11},{10,... | collective-permute-start | bytes 196616 | tf_op jit(solution)/shard_map/ppermute | solution.py:501
  125.4 29.0 %collective-permute-start.8 = (bf16[16,2048]{1,0:T(8,128)(2,1)S(1)}, bf16[16,2048]{1,0:T(8,128)(2,1)S(1)}, u32[]{:S(2)}, u32[]{:S(2)}) collective-permute-start(bf16[16,2048]{1,0:T(8,128)(2,1)S(1)} %reduce_sum.12.refs_4_), channel_id=1, source_target_pairs={{0,3},{1,0},{2,1},{3,2},{4,7},{5,4},{6,5},{7,6},{8,11},{9,8},{10,9... | collective-permute-start | bytes 196616 | tf_op jit(solution)/shard_map/ppermute | solution.py:501
  127.1 27.3 %copy-start = (bf16[1024,512]{1,0:T(8,128)(2,1)S(1)}, bf16[1024,512]{1,0:T(8,128)(2,1)}, u32[]{:S(2)}) copy-start(bf16[1024,512]{1,0:T(8,128)(2,1)} %in_w_ref.3) | copy-start | bytes 3145732
  127.1 27.3 %copy-start.2 = (bf16[10,1024]{1,0:T(8,128)(2,1)S(1)}, bf16[10,1024]{1,0:T(8,128)(2,1)}, u32[]{:S(2)}) copy-start(bf16[10,1024]{1,0:T(8,128)(2,1)} %embed_ref.3) | copy-start | bytes 61444
  127.1 27.3 %copy-start.3 = (f32[16,512]{1,0:T(8,128)S(1)}, f32[16,512]{1,0:T(8,128)}, u32[]{:S(2)}) copy-start(f32[16,512]{1,0:T(8,128)} %get-tuple-element.31.tanh_ref) | copy-start | bytes 98308

commit v2 on v1

--- a/solution.py
+++ b/solution.py
@@ -12,6 +12,7 @@
 PREFIX = 10
 PAD = 16
 SHORT = 256
+PAD_BITS, HEAD_DIM_BITS, SHORT_BITS = 4, 6, 8
 BLK = 256
 QUAD = 4 * HEAD_DIM
 QUADS = HEADS // 4
@@ -65,16 +66,16 @@
 
 
 def quad_prefix(prefix, quad):
-    row = lax.broadcasted_iota(jnp.int32, (128, QUAD), 0) // PAD
-    col = lax.broadcasted_iota(jnp.int32, (128, QUAD), 1) // HEAD_DIM
+    row = lax.broadcasted_iota(jnp.int32, (128, QUAD), 0) >> PAD_BITS
+    col = lax.broadcasted_iota(jnp.int32, (128, QUAD), 1) >> HEAD_DIM_BITS
     tiled = jnp.concatenate([prefix] * 8, axis=0)
     return jnp.where(row == col + 4 * (quad % 2), tiled, jnp.zeros_like(tiled))
 
 
 def full_prefix(prefix):
     shape = (HEADS * PAD, D)
-    row = lax.broadcasted_iota(jnp.int32, shape, 0) // PAD
-    col = lax.broadcasted_iota(jnp.int32, shape, 1) // HEAD_DIM
+    row = lax.broadcasted_iota(jnp.int32, shape, 0) >> PAD_BITS
+    col = lax.broadcasted_iota(jnp.int32, shape, 1) >> HEAD_DIM_BITS
     tiled = jnp.concatenate([prefix] * HEADS, axis=0)
     return jnp.where(row == col, tiled, jnp.zeros_like(tiled))
 
@@ -129,7 +130,7 @@
 
 def live_column(bucket_ref, lens_ref, first, rows, slots):
     position = lax.broadcasted_iota(jnp.int32, (rows, 1), 0) + first
-    segment = position // SHORT
+    segment = position >> SHORT_BITS
     total = jnp.int32(0)
     short_len = jnp.zeros((rows, 1), jnp.int32)
     for index in range(slots // SHORT):
@@ -153,8 +154,8 @@
     prefix_vals = quad_prefix(prefix_ref[:, pl.ds(pl.multiple_of(D + quad * QUAD, QUAD), QUAD)], quad)
     causal = lax.broadcasted_iota(jnp.int32, (BLK, BLK), 1) <= lax.broadcasted_iota(jnp.int32, (BLK, BLK), 0)
     lane = lax.broadcasted_iota(jnp.int32, (BLK, 128), 1)
-    lane_head = lane // PAD - 4 * (quad % 2)
-    lane_real = lane % PAD < PREFIX
+    lane_head = (lane >> PAD_BITS) - 4 * (quad % 2)
+    lane_real = (lane & (PAD - 1)) < PREFIX
 
     def scores(block, head):
         pair = slice(128 * (head // 2), 128 * (head // 2) + 128)
@@ -235,8 +236,8 @@
             owner = (place_ref[0] + (len(pieces) - shift)) % len(pieces)
             prefix_ref[:, pl.ds(pl.multiple_of(owner * width, 128), width)] = piece[...]
         vp_ref[...] = full_prefix(prefix_ref[:, D:])
-        row = lax.broadcasted_iota(jnp.int32, (D, HEADS * PAD), 0) // HEAD_DIM
-        col = lax.broadcasted_iota(jnp.int32, (D, HEADS * PAD), 1) // PAD
+        row = lax.broadcasted_iota(jnp.int32, (D, HEADS * PAD), 0) >> HEAD_DIM_BITS
+        col = lax.broadcasted_iota(jnp.int32, (D, HEADS * PAD), 1) >> PAD_BITS
         spread_ref[...] = jnp.where(row == col, 1.0, 0.0).astype(BF)
         bias_ref[...] = row_of(fc_b_ref)
         d_kp_ref[...] = jnp.zeros_like(d_kp_ref)
@@ -296,7 +297,7 @@
 
         chunks = FF // CHUNK
         pre_ref[...], d_act_ref[...] = opened(0)
-        lax.fori_loop(0, chunks - 1, chunk_step, 0)
+        lax.fori_loop(0, chunks - 1, chunk_step, 0, unroll=True)
         result, d_normed = closed(chunks - 1, pre_ref[...], d_act_ref[...])
         block_ref[...] = jnp.where(live, result, 0.0).astype(BF)
         d_mid = grad_out_ref[...].astype(F32) + norm_back(d_normed * row_of(gain_ref), norm_ref[...], inv)
@@ -317,8 +318,8 @@
     def _():
         shape = (HEADS * PAD, D)
         own = (
-            lax.broadcasted_iota(jnp.int32, shape, 0) // PAD
-            == lax.broadcasted_iota(jnp.int32, shape, 1) // HEAD_DIM
+            lax.broadcasted_iota(jnp.int32, shape, 0) >> PAD_BITS
+            == lax.broadcasted_iota(jnp.int32, shape, 1) >> HEAD_DIM_BITS
         )
         for index, ref in enumerate((d_kp_ref, d_vp_ref)):
             kept = jnp.where(own, ref[...], 0.0)
@@ -341,8 +342,8 @@
 ):
     causal = lax.broadcasted_iota(jnp.int32, (BLK, BLK), 0) <= lax.broadcasted_iota(jnp.int32, (BLK, BLK), 1)
     left = head_mask((BLK, 128), 0)
-    row = lax.broadcasted_iota(jnp.int32, (128, 128), 0) // PAD
-    col = lax.broadcasted_iota(jnp.int32, (128, 128), 1) // HEAD_DIM
+    row = lax.broadcasted_iota(jnp.int32, (128, 128), 0) >> PAD_BITS
+    col = lax.broadcasted_iota(jnp.int32, (128, 128), 1) >> HEAD_DIM_BITS
     tiled = jnp.concatenate([pk_ref[...]] * 8, axis=0)
     prefix_keys = jnp.where(row == col + 2 * (pair % 4), tiled, jnp.zeros_like(tiled))
 
@@ -544,9 +545,6 @@
         cost_estimate=cost(6 * slots * D * D, 16 * 2**20),
         name="project",
     )(x, ln1_gain, ln1_shift, qkv_bias, qkv_weight)
-    late_weight, _ = lax.optimization_barrier((reparam_out, mixed))
-    weight_pieces = to_all(late_weight, "rep")
-
     def quad_at(offset):
         return pl.BlockSpec((slots, QUAD), lambda g: (0, offset + jnp.minimum(g, QUADS - 1)))
 
@@ -602,7 +600,7 @@
             pltpu.SemaphoreType.DMA((3,)),
             pltpu.SemaphoreType.DMA,
         ],
-        compiler_params=params(60),
+        compiler_params=params(56),
         cost_estimate=cost(50e9, 40 * 2**20),
         name="forward",
     )(
@@ -610,6 +608,8 @@
         out_weight, fc_weight, proj_weight, *prefix_pieces,
     )
 
+    late_weight, _ = lax.optimization_barrier((reparam_out, prefix_rows))
+    weight_pieces = to_all(late_weight, "rep")
     batch_rows = lax.all_to_all(prefix_rows, "batch", split_axis=0, concat_axis=0, tiled=True)
 
     pairs = HEADS // 2

time: 158 us -> 155 us (0.981)
  the two profiles are of different devices: /device:TPU:0 before, /device:TPU:2 now
where the time goes in v2:
time: 155 us; the launch traced here: 154 us
  Pallas kernels  138 us (89%)
  starting transfers between devices  14.4 us (9%)
    pallas_call x1, Pallas kernels, local(): pl.pallas_call(forward_kernel, grid=(QUADS + blocks,), out_shape=(shape((...  76.5 us
    pallas_call x1, Pallas kernels, local(): pl.pallas_call(backward_kernel, grid=(late + blocks,), out_shape=shape((s...  27.2 us
    pallas_call x1, Pallas kernels, local(): pl.pallas_call(early_back_kernel, grid=(early,), out_shape=shape((3, slot...  17.3 us
    pallas_call x1, Pallas kernels, local(): pl.pallas_call(project_kernel, grid=(3,), out_shape=shape((slots, 3 * D),...  11.9 us
    ppermute x9, starting transfers between devices, to_all(): lax.ppermute(value, axis, [(place, (place + shift) % size) for place in r...  8.02 us
    all_to_all x1, starting transfers between devices, local(): lax.all_to_all(prefix_rows, 'batch', split_axis=0, concat_axis=0, tiled=T...  6.34 us
  transfers between devices with their start and end apart: 10, of which 0 were waited for; matrix products, arithmetic and copies ran while one was open for 0% of the time, Pallas kernels for 37%

profile of v2, /device:TPU:2, one launch (start us, length us, event | category | flops | bytes accessed | tf_op | source)
XLA Modules:
  0.0 154.5 jit_solution(3584817343831660167)
XLA Ops:
  0.6 2.4 %reparam.1 = (f32[16,512]{1,0:T(8,128)}, bf16[16,512]{1,0:T(8,128)(2,1)}) custom-call(bf16[10,1024]{1,0:T(8,128)(2,1)} %embed_ref.3, bf16[1024,512]{1,0:T(8,128)(2,1)} %in_w_ref.3, bf16[512]{0:T(512)(128)(2,1)} %in_b_ref.1, bf16[512,512]{1,0:T(8,128)(2,1)} %refs_0_, bf16[512]{0:T(512)(128)(2,1)} %out_b_ref.2), custom_call_target="tpu_custom_call" | custom-call | tf_op jit(solution)/shard_map/reparam/pallas_call | solution.py:521
  3.0 0.0 collective-permute-start
  3.0 1.6 %collective-permute-start.1 = (bf16[16,512]{1,0:T(8,128)(2,1)}, bf16[16,512]{1,0:T(8,128)(2,1)S(1)}, u32[]{:S(2)}, u32[]{:S(2)}) collective-permute-start(bf16[16,512]{1,0:T(8,128)(2,1)} %get-tuple-element.23.refs_0_), channel_id=1, source_target_pairs={{0,2},{1,3},{2,0},{3,1},{4,6},{5,7},{6,4},{7,5},{8,10},{9,11},{10,... | collective-permute-start | bytes 49160 | tf_op jit(solution)/shard_map/ppermute | solution.py:502
  4.6 1.4 collective-permute-start.2
  6.0 11.9 %project.1.q_ref.k_ref.v_ref.q_rows_ref.refs_0_.refs_1_.refs_2_ = bf16[1024,3072]{1,0:T(8,128)(2,1)} custom-call(bf16[1024,1024]{1,0:T(8,128)(2,1)} %bitcast.8, bf16[1024]{0:T(1024)(128)(2,1)} %refs_11_.1, bf16[1024]{0:T(1024)(128)(2,1)} %shift_ref.2, bf16[3072]{0:T(1024)(128)(2,1)} %bias_ref.1, bf16[1024,3072]{1,0:T(8,128)(2,1)} %refs_12_.1), custom_call_target="tpu_custom_call" | custom-call | flops 6442450944 | bytes 16777216 | tf_op jit(solution)/shard_map/project/pallas_call | solution.py:533
  18.6 0.0 collective-permute-done.refs_1_
  18.6 0.0 copy-start.4
  18.6 0.0 collective-permute-done.1.refs_2_
  18.6 0.0 copy-start.5
  18.6 0.0 collective-permute-done.2.refs_3_
  18.6 0.0 copy-start.6
  18.6 0.5 copy-done.4
  19.2 0.0 copy-done.5
  19.2 0.0 copy-done.6
  19.2 0.0 copy-start.1
  19.2 76.5 %forward.1 = (bf16[1024,1024]{1,0:T(8,128)(2,1)}, f32[1024,1024]{1,0:T(8,128)}, bf16[1024,1024]{1,0:T(8,128)(2,1)}, bf16[1024,256]{1,0:T(8,128)(2,1)}, f32[256,1...) custom-call(s32[1]{0:T(128)} %bitcast.place_ref, ...), custom_call_target="tpu_custom_call" | custom-call | flops 49999998976 | bytes 41943040 | tf_op jit(solution)/shard_map/forward/pallas_call | solution.py:558
  95.8 0.0 copy-done.1
  95.8 0.1 collective-permute-start.3
  95.8 0.6 collective-permute-start.4
  96.4 1.4 collective-permute-start.5
  97.8 6.3 %all-to-all-start = ((bf16[8,16,2048]{2,1,0:T(8,128)(2,1)}), bf16[8,16,2048]{2,1,0:T(8,128)(2,1)S(1)}, u32[]{:S(2)}, u32[]{:S(2)}) async-start(bf16[8,16,2048]{2,1,0:T(8,128)(2,1)} %get-tuple-element.32), calls=%async_computation | async-start | bytes 1048576 | tf_op jit(solution)/shard_map/all_to_all | solution.py:613
  104.1 17.3 %early_back.1.refs_8_ = bf16[3,1024,512]{2,1,0:T(8,128)(2,1)} custom-call(s32[1]{0:T(128)S(6)} %copy.28.bucket_ref, bf16[1024,3072]{1,0:T(8,128)(2,1)} %project.1.q_ref.k_ref.v_ref.q_rows_ref.refs_0_.refs_1_.refs_2_, bf16[1024,3072]{1,0:T(8,128)(2,1)} %project.1.q_ref.k_ref.v_ref.q_rows_ref.refs_0_.refs_1_.refs_2_, ...), custom_call_target="tpu_custom_call" | custom-call | flops 14000000000 | bytes 10485760 | tf_op jit(solution)/shard_map/early_back/pallas_call | solution.py:635
  121.4 0.0 all-to-all-done
  121.5 0.1 reduce_sum.12.refs_4_
  121.5 0.1 collective-permute-start.6
  121.6 1.6 %collective-permute-start.7 = (bf16[16,2048]{1,0:T(8,128)(2,1)S(1)}, bf16[16,2048]{1,0:T(8,128)(2,1)S(1)}, u32[]{:S(2)}, u32[]{:S(2)}) collective-permute-start(bf16[16,2048]{1,0:T(8,128)(2,1)S(1)} %reduce_sum.12.refs_4_), channel_id=1, source_target_pairs={{0,2},{1,3},{2,0},{3,1},{4,6},{5,7},{6,4},{7,5},{8,10},{9,11},{10,... | collective-permute-start | bytes 196616 | tf_op jit(solution)/shard_map/ppermute | solution.py:502
  123.2 0.0 collective-permute-done.3.refs_1_
  123.2 1.4 collective-permute-start.8
  124.6 0.0 copy-start
  124.6 0.0 copy-start.2
  124.6 0.0 copy-start.3
  124.6 27.2 %backward.1 = bf16[1024,1024]{1,0:T(8,128)(2,1)} custom-call(s32[1]{0:T(128)S(6)} %copy.28.bucket_ref, bf16[1024,3072]{1,0:T(8,128)(2,1)} %project.1.q_ref.k_ref.v_ref.q_rows_ref.refs_0_.refs_1_.refs_2_, bf16[1024,3072]{1,0:T(8,128)(2,1)} %project.1.q_ref.k_ref.v_ref.q_rows_ref.refs_0_.refs_1_.refs_2_, ...), custom_call_target="tpu_custom_call" | custom-call | flops 24000000000 | bytes 31457280 | tf_op jit(solution)/shard_map/backward/pallas_call | solution.py:651
  151.8 0.0 collective-permute-done.4.refs_2_
  151.8 0.0 collective-permute-done.5.refs_3_
  151.8 0.0 collective-permute-done.6.refs_5_
  151.8 0.0 collective-permute-done.7.refs_6_
  151.9 0.0 collective-permute-done.8.refs_7_
  151.9 0.0 copy-done
  151.9 0.0 copy-done.2
  151.9 0.0 copy-done.3
  151.9 2.6 %tail.1 = (f32[10,1024]{1,0:T(8,128)}, f32[1024,512]{1,0:T(8,128)}, f32[1,512]{1,0:T(1,128)}, f32[512,512]{1,0:T(8,128)}, f32[1,512]{1,0:T(1,128)}) custom-call(s32[1]{0:T(128)} %bitcast.place_ref, f32[16,512]{1,0:T(8,128)S(1)} %copy-done.3, bf16[10,1024]{1,0:T(8,128)(2,1)S(1)} %copy-done.2, bf16[1024,512]{1,0:T(8,128)(2,1)S(1)} %copy-done, ...), custom_call_target="tpu_custom_call" | custom-call | tf_op jit(solution)/shard_map/tail/pallas_call | solution.py:679
Async XLA Ops:
  3.0 15.6 %collective-permute-start = (bf16[16,512]{1,0:T(8,128)(2,1)}, bf16[16,512]{1,0:T(8,128)(2,1)S(1)}, u32[]{:S(2)}, u32[]{:S(2)}) collective-permute-start(bf16[16,512]{1,0:T(8,128)(2,1)} %get-tuple-element.23.refs_0_), channel_id=1, source_target_pairs={{0,1},{1,2},{2,3},{3,0},{4,5},{5,6},{6,7},{7,4},{8,9},{9,10},{10,1... | collective-permute-start | bytes 49160 | tf_op jit(solution)/shard_map/ppermute | solution.py:502
  3.0 15.6 %collective-permute-start.1 = (bf16[16,512]{1,0:T(8,128)(2,1)}, bf16[16,512]{1,0:T(8,128)(2,1)S(1)}, u32[]{:S(2)}, u32[]{:S(2)}) collective-permute-start(bf16[16,512]{1,0:T(8,128)(2,1)} %get-tuple-element.23.refs_0_), channel_id=1, source_target_pairs={{0,2},{1,3},{2,0},{3,1},{4,6},{5,7},{6,4},{7,5},{8,10},{9,11},{10,... | collective-permute-start | bytes 49160 | tf_op jit(solution)/shard_map/ppermute | solution.py:502
  4.6 14.1 %collective-permute-start.2 = (bf16[16,512]{1,0:T(8,128)(2,1)}, bf16[16,512]{1,0:T(8,128)(2,1)S(1)}, u32[]{:S(2)}, u32[]{:S(2)}) collective-permute-start(bf16[16,512]{1,0:T(8,128)(2,1)} %get-tuple-element.23.refs_0_), channel_id=1, source_target_pairs={{0,3},{1,0},{2,1},{3,2},{4,7},{5,4},{6,5},{7,6},{8,11},{9,8},{10,9... | collective-permute-start | bytes 49160 | tf_op jit(solution)/shard_map/ppermute | solution.py:502
  18.6 0.6 copy-start.4
  18.6 0.6 copy-start.5
  18.6 0.6 copy-start.6
  19.2 76.5 %copy-start.1 = (bf16[512,512]{1,0:T(8,128)(2,1)S(1)}, bf16[512,512]{1,0:T(8,128)(2,1)}, u32[]{:S(2)}) copy-start(bf16[512,512]{1,0:T(8,128)(2,1)} %refs_0_) | copy-start | bytes 1572868
  95.8 27.4 %collective-permute-start.3 = (bf16[512,512]{1,0:T(8,128)(2,1)S(1)}, bf16[512,512]{1,0:T(8,128)(2,1)S(1)}, u32[]{:S(2)}, u32[]{:S(2)}) collective-permute-start(bf16[512,512]{1,0:T(8,128)(2,1)S(1)} %copy-done.1), channel_id=1, source_target_pairs={{0,1},{1,2},{2,3},{3,0},{4,5},{5,6},{6,7},{7,4},{8,9},{9,10},{10,1... | collective-permute-start | bytes 1572872 | tf_op jit(solution)/shard_map/ppermute | solution.py:502
  95.8 56.0 %collective-permute-start.4 = (bf16[512,512]{1,0:T(8,128)(2,1)S(1)}, bf16[512,512]{1,0:T(8,128)(2,1)S(1)}, u32[]{:S(2)}, u32[]{:S(2)}) collective-permute-start(bf16[512,512]{1,0:T(8,128)(2,1)S(1)} %copy-done.1), channel_id=1, source_target_pairs={{0,2},{1,3},{2,0},{3,1},{4,6},{5,7},{6,4},{7,5},{8,10},{9,11},{10,... | collective-permute-start | bytes 1572872 | tf_op jit(solution)/shard_map/ppermute | solution.py:502
  96.4 55.4 %collective-permute-start.5 = (bf16[512,512]{1,0:T(8,128)(2,1)S(1)}, bf16[512,512]{1,0:T(8,128)(2,1)S(1)}, u32[]{:S(2)}, u32[]{:S(2)}) collective-permute-start(bf16[512,512]{1,0:T(8,128)(2,1)S(1)} %copy-done.1), channel_id=1, source_target_pairs={{0,3},{1,0},{2,1},{3,2},{4,7},{5,4},{6,5},{7,6},{8,11},{9,8},{10,9... | collective-permute-start | bytes 1572872 | tf_op jit(solution)/shard_map/ppermute | solution.py:502
  97.8 23.6 %all-to-all-start = ((bf16[8,16,2048]{2,1,0:T(8,128)(2,1)}), bf16[8,16,2048]{2,1,0:T(8,128)(2,1)S(1)}, u32[]{:S(2)}, u32[]{:S(2)}) async-start(bf16[8,16,2048]{2,1,0:T(8,128)(2,1)} %get-tuple-element.32), calls=%async_computation | async-start | bytes 1048576 | tf_op jit(solution)/shard_map/all_to_all | solution.py:613
  121.5 30.3 %collective-permute-start.6 = (bf16[16,2048]{1,0:T(8,128)(2,1)S(1)}, bf16[16,2048]{1,0:T(8,128)(2,1)S(1)}, u32[]{:S(2)}, u32[]{:S(2)}) collective-permute-start(bf16[16,2048]{1,0:T(8,128)(2,1)S(1)} %reduce_sum.12.refs_4_), channel_id=1, source_target_pairs={{0,1},{1,2},{2,3},{3,0},{4,5},{5,6},{6,7},{7,4},{8,9},{9,10},{10,1... | collective-permute-start | bytes 196616 | tf_op jit(solution)/shard_map/ppermute | solution.py:502
  121.6 30.2 %collective-permute-start.7 = (bf16[16,2048]{1,0:T(8,128)(2,1)S(1)}, bf16[16,2048]{1,0:T(8,128)(2,1)S(1)}, u32[]{:S(2)}, u32[]{:S(2)}) collective-permute-start(bf16[16,2048]{1,0:T(8,128)(2,1)S(1)} %reduce_sum.12.refs_4_), channel_id=1, source_target_pairs={{0,2},{1,3},{2,0},{3,1},{4,6},{5,7},{6,4},{7,5},{8,10},{9,11},{10,... | collective-permute-start | bytes 196616 | tf_op jit(solution)/shard_map/ppermute | solution.py:502
  123.2 28.7 %collective-permute-start.8 = (bf16[16,2048]{1,0:T(8,128)(2,1)S(1)}, bf16[16,2048]{1,0:T(8,128)(2,1)S(1)}, u32[]{:S(2)}, u32[]{:S(2)}) collective-permute-start(bf16[16,2048]{1,0:T(8,128)(2,1)S(1)} %reduce_sum.12.refs_4_), channel_id=1, source_target_pairs={{0,3},{1,0},{2,1},{3,2},{4,7},{5,4},{6,5},{7,6},{8,11},{9,8},{10,9... | collective-permute-start | bytes 196616 | tf_op jit(solution)/shard_map/ppermute | solution.py:502
  124.6 27.3 %copy-start = (bf16[1024,512]{1,0:T(8,128)(2,1)S(1)}, bf16[1024,512]{1,0:T(8,128)(2,1)}, u32[]{:S(2)}) copy-start(bf16[1024,512]{1,0:T(8,128)(2,1)} %in_w_ref.3) | copy-start | bytes 3145732
  124.6 27.3 %copy-start.2 = (bf16[10,1024]{1,0:T(8,128)(2,1)S(1)}, bf16[10,1024]{1,0:T(8,128)(2,1)}, u32[]{:S(2)}) copy-start(bf16[10,1024]{1,0:T(8,128)(2,1)} %embed_ref.3) | copy-start | bytes 61444
  124.6 27.3 %copy-start.3 = (f32[16,512]{1,0:T(8,128)S(1)}, f32[16,512]{1,0:T(8,128)}, u32[]{:S(2)}) copy-start(f32[16,512]{1,0:T(8,128)} %get-tuple-element.31.tanh_ref) | copy-start | bytes 98308

commit v3 on v2

--- a/solution.py
+++ b/solution.py
@@ -166,7 +166,7 @@
         return own if raw.shape[1] == BLK else jnp.concatenate([raw[:, :-BLK], own], axis=1)
 
     units = [(block, head) for block in query_blocks for head in range(4)]
-    ahead = 2
+    ahead = 1
     queue = [scores(*unit) for unit in units[:ahead]]
     for index, (block, head) in enumerate(units):
         if index + ahead < len(units):

time: 155 us -> 154 us (level)
  the two profiles are of different devices: /device:TPU:2 before, /device:TPU:0 now
where the time goes in v3:
time: 154 us; the launch traced here: 155 us
  Pallas kernels  137 us (89%)
  starting transfers between devices  15.3 us (10%)
    pallas_call x1, Pallas kernels, local(): pl.pallas_call(forward_kernel, grid=(QUADS + blocks,), out_shape=(shape((...  75.8 us
    pallas_call x1, Pallas kernels, local(): pl.pallas_call(backward_kernel, grid=(late + blocks,), out_shape=shape((s...  27.2 us
    pallas_call x1, Pallas kernels, local(): pl.pallas_call(early_back_kernel, grid=(early,), out_shape=shape((3, slot...  17.3 us
    pallas_call x1, Pallas kernels, local(): pl.pallas_call(project_kernel, grid=(3,), out_shape=shape((slots, 3 * D),...  11.9 us
    ppermute x9, starting transfers between devices, to_all(): lax.ppermute(value, axis, [(place, (place + shift) % size) for place in r...  9.49 us
    all_to_all x1, starting transfers between devices, local(): lax.all_to_all(prefix_rows, 'batch', split_axis=0, concat_axis=0, tiled=T...  5.79 us
  transfers between devices with their start and end apart: 10, of which 0 were waited for; matrix products, arithmetic and copies ran while one was open for 0% of the time, Pallas kernels for 37%

profile of v3, /device:TPU:0, one launch (start us, length us, event | category | flops | bytes accessed | tf_op | source)
XLA Modules:
  0.0 154.6 jit_solution(4301426021037477346)
XLA Ops:
  0.6 2.4 %reparam.1 = (f32[16,512]{1,0:T(8,128)}, bf16[16,512]{1,0:T(8,128)(2,1)}) custom-call(bf16[10,1024]{1,0:T(8,128)(2,1)} %embed_ref.3, bf16[1024,512]{1,0:T(8,128)(2,1)} %in_w_ref.3, bf16[512]{0:T(512)(128)(2,1)} %in_b_ref.1, bf16[512,512]{1,0:T(8,128)(2,1)} %refs_0_, bf16[512]{0:T(512)(128)(2,1)} %out_b_ref.2), custom_call_target="tpu_custom_call" | custom-call | tf_op jit(solution)/shard_map/reparam/pallas_call | solution.py:521
  3.0 0.5 collective-permute-start
  3.5 2.5 %collective-permute-start.1 = (bf16[16,512]{1,0:T(8,128)(2,1)}, bf16[16,512]{1,0:T(8,128)(2,1)S(1)}, u32[]{:S(2)}, u32[]{:S(2)}) collective-permute-start(bf16[16,512]{1,0:T(8,128)(2,1)} %get-tuple-element.23.refs_0_), channel_id=1, source_target_pairs={{0,2},{1,3},{2,0},{3,1},{4,6},{5,7},{6,4},{7,5},{8,10},{9,11},{10,... | collective-permute-start | bytes 49160 | tf_op jit(solution)/shard_map/ppermute | solution.py:502
  6.0 1.4 collective-permute-start.2
  7.4 11.9 %project.1.q_ref.k_ref.v_ref.q_rows_ref.refs_0_.refs_1_.refs_2_ = bf16[1024,3072]{1,0:T(8,128)(2,1)} custom-call(bf16[1024,1024]{1,0:T(8,128)(2,1)} %bitcast.8, bf16[1024]{0:T(1024)(128)(2,1)} %refs_11_.1, bf16[1024]{0:T(1024)(128)(2,1)} %shift_ref.2, bf16[3072]{0:T(1024)(128)(2,1)} %bias_ref.1, bf16[1024,3072]{1,0:T(8,128)(2,1)} %refs_12_.1), custom_call_target="tpu_custom_call" | custom-call | flops 6442450944 | bytes 16777216 | tf_op jit(solution)/shard_map/project/pallas_call | solution.py:533
  20.0 0.0 collective-permute-done.refs_1_
  20.0 0.0 copy-start.4
  20.1 0.0 collective-permute-done.1.refs_2_
  20.1 0.0 copy-start.5
  20.1 0.0 collective-permute-done.2.refs_3_
  20.1 0.0 copy-start.6
  20.1 0.5 copy-done.4
  20.6 0.0 copy-done.5
  20.7 0.0 copy-done.6
  20.7 0.0 copy-start.1
  20.7 75.8 %forward.1 = (bf16[1024,1024]{1,0:T(8,128)(2,1)}, f32[1024,1024]{1,0:T(8,128)}, bf16[1024,1024]{1,0:T(8,128)(2,1)}, bf16[1024,256]{1,0:T(8,128)(2,1)}, f32[256,1...) custom-call(s32[1]{0:T(128)} %bitcast.place_ref, ...), custom_call_target="tpu_custom_call" | custom-call | flops 49999998976 | bytes 41943040 | tf_op jit(solution)/shard_map/forward/pallas_call | solution.py:558
  96.5 0.0 copy-done.1
  96.5 0.1 collective-permute-start.3
  96.5 0.4 collective-permute-start.4
  96.9 1.4 collective-permute-start.5
  98.3 5.8 %all-to-all-start = ((bf16[8,16,2048]{2,1,0:T(8,128)(2,1)}), bf16[8,16,2048]{2,1,0:T(8,128)(2,1)S(1)}, u32[]{:S(2)}, u32[]{:S(2)}) async-start(bf16[8,16,2048]{2,1,0:T(8,128)(2,1)} %get-tuple-element.32), calls=%async_computation | async-start | bytes 1048576 | tf_op jit(solution)/shard_map/all_to_all | solution.py:613
  104.1 17.3 %early_back.1.refs_8_ = bf16[3,1024,512]{2,1,0:T(8,128)(2,1)} custom-call(s32[1]{0:T(128)S(6)} %copy.28.bucket_ref, bf16[1024,3072]{1,0:T(8,128)(2,1)} %project.1.q_ref.k_ref.v_ref.q_rows_ref.refs_0_.refs_1_.refs_2_, bf16[1024,3072]{1,0:T(8,128)(2,1)} %project.1.q_ref.k_ref.v_ref.q_rows_ref.refs_0_.refs_1_.refs_2_, ...), custom_call_target="tpu_custom_call" | custom-call | flops 14000000000 | bytes 10485760 | tf_op jit(solution)/shard_map/early_back/pallas_call | solution.py:635
  121.4 0.0 all-to-all-done
  121.4 0.1 reduce_sum.12.refs_4_
  121.5 0.1 collective-permute-start.6
  121.6 1.8 %collective-permute-start.7 = (bf16[16,2048]{1,0:T(8,128)(2,1)S(1)}, bf16[16,2048]{1,0:T(8,128)(2,1)S(1)}, u32[]{:S(2)}, u32[]{:S(2)}) collective-permute-start(bf16[16,2048]{1,0:T(8,128)(2,1)S(1)} %reduce_sum.12.refs_4_), channel_id=1, source_target_pairs={{0,2},{1,3},{2,0},{3,1},{4,6},{5,7},{6,4},{7,5},{8,10},{9,11},{10,... | collective-permute-start | bytes 196616 | tf_op jit(solution)/shard_map/ppermute | solution.py:502
  123.3 0.0 collective-permute-done.3.refs_1_
  123.3 1.4 collective-permute-start.8
  124.7 0.0 copy-start
  124.7 0.0 copy-start.2
  124.7 0.0 copy-start.3
  124.7 27.2 %backward.1 = bf16[1024,1024]{1,0:T(8,128)(2,1)} custom-call(s32[1]{0:T(128)S(6)} %copy.28.bucket_ref, bf16[1024,3072]{1,0:T(8,128)(2,1)} %project.1.q_ref.k_ref.v_ref.q_rows_ref.refs_0_.refs_1_.refs_2_, bf16[1024,3072]{1,0:T(8,128)(2,1)} %project.1.q_ref.k_ref.v_ref.q_rows_ref.refs_0_.refs_1_.refs_2_, ...), custom_call_target="tpu_custom_call" | custom-call | flops 24000000000 | bytes 31457280 | tf_op jit(solution)/shard_map/backward/pallas_call | solution.py:651
  152.0 0.0 collective-permute-done.4.refs_2_
  152.0 0.0 collective-permute-done.5.refs_3_
  152.0 0.0 collective-permute-done.6.refs_5_
  152.0 0.0 collective-permute-done.7.refs_6_
  152.0 0.0 collective-permute-done.8.refs_7_
  152.0 0.0 copy-done
  152.0 0.0 copy-done.2
  152.1 0.0 copy-done.3
  152.1 2.6 %tail.1 = (f32[10,1024]{1,0:T(8,128)}, f32[1024,512]{1,0:T(8,128)}, f32[1,512]{1,0:T(1,128)}, f32[512,512]{1,0:T(8,128)}, f32[1,512]{1,0:T(1,128)}) custom-call(s32[1]{0:T(128)} %bitcast.place_ref, f32[16,512]{1,0:T(8,128)S(1)} %copy-done.3, bf16[10,1024]{1,0:T(8,128)(2,1)S(1)} %copy-done.2, bf16[1024,512]{1,0:T(8,128)(2,1)S(1)} %copy-done, ...), custom_call_target="tpu_custom_call" | custom-call | tf_op jit(solution)/shard_map/tail/pallas_call | solution.py:679
Async XLA Ops:
  3.0 17.0 %collective-permute-start = (bf16[16,512]{1,0:T(8,128)(2,1)}, bf16[16,512]{1,0:T(8,128)(2,1)S(1)}, u32[]{:S(2)}, u32[]{:S(2)}) collective-permute-start(bf16[16,512]{1,0:T(8,128)(2,1)} %get-tuple-element.23.refs_0_), channel_id=1, source_target_pairs={{0,1},{1,2},{2,3},{3,0},{4,5},{5,6},{6,7},{7,4},{8,9},{9,10},{10,1... | collective-permute-start | bytes 49160 | tf_op jit(solution)/shard_map/ppermute | solution.py:502
  3.5 16.6 %collective-permute-start.1 = (bf16[16,512]{1,0:T(8,128)(2,1)}, bf16[16,512]{1,0:T(8,128)(2,1)S(1)}, u32[]{:S(2)}, u32[]{:S(2)}) collective-permute-start(bf16[16,512]{1,0:T(8,128)(2,1)} %get-tuple-element.23.refs_0_), channel_id=1, source_target_pairs={{0,2},{1,3},{2,0},{3,1},{4,6},{5,7},{6,4},{7,5},{8,10},{9,11},{10,... | collective-permute-start | bytes 49160 | tf_op jit(solution)/shard_map/ppermute | solution.py:502
  6.0 14.1 %collective-permute-start.2 = (bf16[16,512]{1,0:T(8,128)(2,1)}, bf16[16,512]{1,0:T(8,128)(2,1)S(1)}, u32[]{:S(2)}, u32[]{:S(2)}) collective-permute-start(bf16[16,512]{1,0:T(8,128)(2,1)} %get-tuple-element.23.refs_0_), channel_id=1, source_target_pairs={{0,3},{1,0},{2,1},{3,2},{4,7},{5,4},{6,5},{7,6},{8,11},{9,8},{10,9... | collective-permute-start | bytes 49160 | tf_op jit(solution)/shard_map/ppermute | solution.py:502
  20.0 0.6 copy-start.4
  20.1 0.6 copy-start.5
  20.1 0.6 copy-start.6
  20.7 75.8 %copy-start.1 = (bf16[512,512]{1,0:T(8,128)(2,1)S(1)}, bf16[512,512]{1,0:T(8,128)(2,1)}, u32[]{:S(2)}) copy-start(bf16[512,512]{1,0:T(8,128)(2,1)} %refs_0_) | copy-start | bytes 1572868
  96.5 26.9 %collective-permute-start.3 = (bf16[512,512]{1,0:T(8,128)(2,1)S(1)}, bf16[512,512]{1,0:T(8,128)(2,1)S(1)}, u32[]{:S(2)}, u32[]{:S(2)}) collective-permute-start(bf16[512,512]{1,0:T(8,128)(2,1)S(1)} %copy-done.1), channel_id=1, source_target_pairs={{0,1},{1,2},{2,3},{3,0},{4,5},{5,6},{6,7},{7,4},{8,9},{9,10},{10,1... | collective-permute-start | bytes 1572872 | tf_op jit(solution)/shard_map/ppermute | solution.py:502
  96.5 55.5 %collective-permute-start.4 = (bf16[512,512]{1,0:T(8,128)(2,1)S(1)}, bf16[512,512]{1,0:T(8,128)(2,1)S(1)}, u32[]{:S(2)}, u32[]{:S(2)}) collective-permute-start(bf16[512,512]{1,0:T(8,128)(2,1)S(1)} %copy-done.1), channel_id=1, source_target_pairs={{0,2},{1,3},{2,0},{3,1},{4,6},{5,7},{6,4},{7,5},{8,10},{9,11},{10,... | collective-permute-start | bytes 1572872 | tf_op jit(solution)/shard_map/ppermute | solution.py:502
  96.9 55.1 %collective-permute-start.5 = (bf16[512,512]{1,0:T(8,128)(2,1)S(1)}, bf16[512,512]{1,0:T(8,128)(2,1)S(1)}, u32[]{:S(2)}, u32[]{:S(2)}) collective-permute-start(bf16[512,512]{1,0:T(8,128)(2,1)S(1)} %copy-done.1), channel_id=1, source_target_pairs={{0,3},{1,0},{2,1},{3,2},{4,7},{5,4},{6,5},{7,6},{8,11},{9,8},{10,9... | collective-permute-start | bytes 1572872 | tf_op jit(solution)/shard_map/ppermute | solution.py:502
  98.3 23.1 %all-to-all-start = ((bf16[8,16,2048]{2,1,0:T(8,128)(2,1)}), bf16[8,16,2048]{2,1,0:T(8,128)(2,1)S(1)}, u32[]{:S(2)}, u32[]{:S(2)}) async-start(bf16[8,16,2048]{2,1,0:T(8,128)(2,1)} %get-tuple-element.32), calls=%async_computation | async-start | bytes 1048576 | tf_op jit(solution)/shard_map/all_to_all | solution.py:613
  121.5 30.5 %collective-permute-start.6 = (bf16[16,2048]{1,0:T(8,128)(2,1)S(1)}, bf16[16,2048]{1,0:T(8,128)(2,1)S(1)}, u32[]{:S(2)}, u32[]{:S(2)}) collective-permute-start(bf16[16,2048]{1,0:T(8,128)(2,1)S(1)} %reduce_sum.12.refs_4_), channel_id=1, source_target_pairs={{0,1},{1,2},{2,3},{3,0},{4,5},{5,6},{6,7},{7,4},{8,9},{9,10},{10,1... | collective-permute-start | bytes 196616 | tf_op jit(solution)/shard_map/ppermute | solution.py:502
  121.6 30.5 %collective-permute-start.7 = (bf16[16,2048]{1,0:T(8,128)(2,1)S(1)}, bf16[16,2048]{1,0:T(8,128)(2,1)S(1)}, u32[]{:S(2)}, u32[]{:S(2)}) collective-permute-start(bf16[16,2048]{1,0:T(8,128)(2,1)S(1)} %reduce_sum.12.refs_4_), channel_id=1, source_target_pairs={{0,2},{1,3},{2,0},{3,1},{4,6},{5,7},{6,4},{7,5},{8,10},{9,11},{10,... | collective-permute-start | bytes 196616 | tf_op jit(solution)/shard_map/ppermute | solution.py:502
  123.3 28.7 %collective-permute-start.8 = (bf16[16,2048]{1,0:T(8,128)(2,1)S(1)}, bf16[16,2048]{1,0:T(8,128)(2,1)S(1)}, u32[]{:S(2)}, u32[]{:S(2)}) collective-permute-start(bf16[16,2048]{1,0:T(8,128)(2,1)S(1)} %reduce_sum.12.refs_4_), channel_id=1, source_target_pairs={{0,3},{1,0},{2,1},{3,2},{4,7},{5,4},{6,5},{7,6},{8,11},{9,8},{10,9... | collective-permute-start | bytes 196616 | tf_op jit(solution)/shard_map/ppermute | solution.py:502
  124.7 27.3 %copy-start = (bf16[1024,512]{1,0:T(8,128)(2,1)S(1)}, bf16[1024,512]{1,0:T(8,128)(2,1)}, u32[]{:S(2)}) copy-start(bf16[1024,512]{1,0:T(8,128)(2,1)} %in_w_ref.3) | copy-start | bytes 3145732
  124.7 27.3 %copy-start.2 = (bf16[10,1024]{1,0:T(8,128)(2,1)S(1)}, bf16[10,1024]{1,0:T(8,128)(2,1)}, u32[]{:S(2)}) copy-start(bf16[10,1024]{1,0:T(8,128)(2,1)} %embed_ref.3) | copy-start | bytes 61444
  124.7 27.3 %copy-start.3 = (f32[16,512]{1,0:T(8,128)S(1)}, f32[16,512]{1,0:T(8,128)}, u32[]{:S(2)}) copy-start(f32[16,512]{1,0:T(8,128)} %get-tuple-element.31.tanh_ref) | copy-start | bytes 98308

commit v4 on v3

--- a/solution.py
+++ b/solution.py
@@ -357,7 +357,7 @@
         return (own if raw.shape[0] == BLK else jnp.concatenate([raw[:-BLK], own], axis=0)), d_prob
 
     units = [(block, side) for block in query_blocks for side in range(2)]
-    ahead = 2
+    ahead = 3
     queue = [opened(*unit) for unit in units[:ahead]]
     d_keys = [[None] * len(query_blocks) for _ in range(2)]
     d_vals = [[None] * len(query_blocks) for _ in range(2)]

time: 154 us -> 153 us (level)
  the two profiles are of different devices: /device:TPU:0 before, /device:TPU:24 now
where the time goes in v4:
time: 153 us; the launch traced here: 152 us
  Pallas kernels  137 us (90%)
  starting transfers between devices  13.1 us (9%)
    pallas_call x1, Pallas kernels, local(): pl.pallas_call(forward_kernel, grid=(QUADS + blocks,), out_shape=(shape((...  75.8 us
    pallas_call x1, Pallas kernels, local(): pl.pallas_call(backward_kernel, grid=(late + blocks,), out_shape=shape((s...  27.2 us
    pallas_call x1, Pallas kernels, local(): pl.pallas_call(early_back_kernel, grid=(early,), out_shape=shape((3, slot...  17.3 us
    pallas_call x1, Pallas kernels, local(): pl.pallas_call(project_kernel, grid=(3,), out_shape=shape((slots, 3 * D),...  11.9 us
    ppermute x9, starting transfers between devices, to_all(): lax.ppermute(value, axis, [(place, (place + shift) % size) for place in r...  7.1 us
    all_to_all x1, starting transfers between devices, local(): lax.all_to_all(prefix_rows, 'batch', split_axis=0, concat_axis=0, tiled=T...  6.03 us
  transfers between devices with their start and end apart: 10, of which 0 were waited for; matrix products, arithmetic and copies ran while one was open for 0% of the time, Pallas kernels for 37%

profile of v4, /device:TPU:24, one launch (start us, length us, event | category | flops | bytes accessed | tf_op | source)
XLA Modules:
  0.0 152.5 jit_solution(3141405676010411639)
XLA Ops:
  0.6 2.4 %reparam.1 = (f32[16,512]{1,0:T(8,128)}, bf16[16,512]{1,0:T(8,128)(2,1)}) custom-call(bf16[10,1024]{1,0:T(8,128)(2,1)} %embed_ref.3, bf16[1024,512]{1,0:T(8,128)(2,1)} %in_w_ref.3, bf16[512]{0:T(512)(128)(2,1)} %in_b_ref.1, bf16[512,512]{1,0:T(8,128)(2,1)} %refs_0_, bf16[512]{0:T(512)(128)(2,1)} %out_b_ref.2), custom_call_target="tpu_custom_call" | custom-call | tf_op jit(solution)/shard_map/reparam/pallas_call | solution.py:521
  3.0 0.0 collective-permute-start
  3.0 1.6 %collective-permute-start.1 = (bf16[16,512]{1,0:T(8,128)(2,1)}, bf16[16,512]{1,0:T(8,128)(2,1)S(1)}, u32[]{:S(2)}, u32[]{:S(2)}) collective-permute-start(bf16[16,512]{1,0:T(8,128)(2,1)} %get-tuple-element.23.refs_0_), channel_id=1, source_target_pairs={{0,2},{1,3},{2,0},{3,1},{4,6},{5,7},{6,4},{7,5},{8,10},{9,11},{10,... | collective-permute-start | bytes 49160 | tf_op jit(solution)/shard_map/ppermute | solution.py:502
  4.6 1.4 collective-permute-start.2
  6.0 11.9 %project.1.q_ref.k_ref.v_ref.q_rows_ref.refs_0_.refs_1_.refs_2_ = bf16[1024,3072]{1,0:T(8,128)(2,1)} custom-call(bf16[1024,1024]{1,0:T(8,128)(2,1)} %bitcast.8, bf16[1024]{0:T(1024)(128)(2,1)} %refs_11_.1, bf16[1024]{0:T(1024)(128)(2,1)} %shift_ref.2, bf16[3072]{0:T(1024)(128)(2,1)} %bias_ref.1, bf16[1024,3072]{1,0:T(8,128)(2,1)} %refs_12_.1), custom_call_target="tpu_custom_call" | custom-call | flops 6442450944 | bytes 16777216 | tf_op jit(solution)/shard_map/project/pallas_call | solution.py:533
  18.6 0.0 collective-permute-done.refs_1_
  18.6 0.0 copy-start.4
  18.6 0.0 collective-permute-done.1.refs_2_
  18.6 0.0 copy-start.5
  18.6 0.0 collective-permute-done.2.refs_3_
  18.6 0.0 copy-start.6
  18.6 0.5 copy-done.4
  19.2 0.0 copy-done.5
  19.2 0.0 copy-done.6
  19.2 0.0 copy-start.1
  19.2 75.8 %forward.1 = (bf16[1024,1024]{1,0:T(8,128)(2,1)}, f32[1024,1024]{1,0:T(8,128)}, bf16[1024,1024]{1,0:T(8,128)(2,1)}, bf16[1024,256]{1,0:T(8,128)(2,1)}, f32[256,1...) custom-call(s32[1]{0:T(128)} %bitcast.place_ref, ...), custom_call_target="tpu_custom_call" | custom-call | flops 49999998976 | bytes 41943040 | tf_op jit(solution)/shard_map/forward/pallas_call | solution.py:558
  95.0 0.0 copy-done.1
  95.0 0.1 collective-permute-start.3
  95.1 0.6 collective-permute-start.4
  95.7 1.4 collective-permute-start.5
  97.0 6.0 %all-to-all-start = ((bf16[8,16,2048]{2,1,0:T(8,128)(2,1)}), bf16[8,16,2048]{2,1,0:T(8,128)(2,1)S(1)}, u32[]{:S(2)}, u32[]{:S(2)}) async-start(bf16[8,16,2048]{2,1,0:T(8,128)(2,1)} %get-tuple-element.32), calls=%async_computation | async-start | bytes 1048576 | tf_op jit(solution)/shard_map/all_to_all | solution.py:613
  103.1 17.3 %early_back.1.refs_8_ = bf16[3,1024,512]{2,1,0:T(8,128)(2,1)} custom-call(s32[1]{0:T(128)S(6)} %copy.28.bucket_ref, bf16[1024,3072]{1,0:T(8,128)(2,1)} %project.1.q_ref.k_ref.v_ref.q_rows_ref.refs_0_.refs_1_.refs_2_, bf16[1024,3072]{1,0:T(8,128)(2,1)} %project.1.q_ref.k_ref.v_ref.q_rows_ref.refs_0_.refs_1_.refs_2_, ...), custom_call_target="tpu_custom_call" | custom-call | flops 14000000000 | bytes 10485760 | tf_op jit(solution)/shard_map/early_back/pallas_call | solution.py:635
  120.4 0.0 all-to-all-done
  120.4 0.1 reduce_sum.12.refs_4_
  120.5 0.1 collective-permute-start.6
  120.5 0.6 collective-permute-start.7
  121.2 0.0 collective-permute-done.3.refs_1_
  121.2 1.4 collective-permute-start.8
  122.6 0.0 copy-start
  122.6 0.0 copy-start.2
  122.6 0.0 copy-start.3
  122.6 27.2 %backward.1 = bf16[1024,1024]{1,0:T(8,128)(2,1)} custom-call(s32[1]{0:T(128)S(6)} %copy.28.bucket_ref, bf16[1024,3072]{1,0:T(8,128)(2,1)} %project.1.q_ref.k_ref.v_ref.q_rows_ref.refs_0_.refs_1_.refs_2_, bf16[1024,3072]{1,0:T(8,128)(2,1)} %project.1.q_ref.k_ref.v_ref.q_rows_ref.refs_0_.refs_1_.refs_2_, ...), custom_call_target="tpu_custom_call" | custom-call | flops 24000000000 | bytes 31457280 | tf_op jit(solution)/shard_map/backward/pallas_call | solution.py:651
  149.8 0.0 collective-permute-done.4.refs_2_
  149.8 0.0 collective-permute-done.5.refs_3_
  149.8 0.0 collective-permute-done.6.refs_5_
  149.9 0.0 collective-permute-done.7.refs_6_
  149.9 0.0 collective-permute-done.8.refs_7_
  149.9 0.0 copy-done
  149.9 0.0 copy-done.2
  149.9 0.0 copy-done.3
  149.9 2.6 %tail.1 = (f32[10,1024]{1,0:T(8,128)}, f32[1024,512]{1,0:T(8,128)}, f32[1,512]{1,0:T(1,128)}, f32[512,512]{1,0:T(8,128)}, f32[1,512]{1,0:T(1,128)}) custom-call(s32[1]{0:T(128)} %bitcast.place_ref, f32[16,512]{1,0:T(8,128)S(1)} %copy-done.3, bf16[10,1024]{1,0:T(8,128)(2,1)S(1)} %copy-done.2, bf16[1024,512]{1,0:T(8,128)(2,1)S(1)} %copy-done, ...), custom_call_target="tpu_custom_call" | custom-call | tf_op jit(solution)/shard_map/tail/pallas_call | solution.py:679
Async XLA Ops:
  3.0 15.6 %collective-permute-start = (bf16[16,512]{1,0:T(8,128)(2,1)}, bf16[16,512]{1,0:T(8,128)(2,1)S(1)}, u32[]{:S(2)}, u32[]{:S(2)}) collective-permute-start(bf16[16,512]{1,0:T(8,128)(2,1)} %get-tuple-element.23.refs_0_), channel_id=1, source_target_pairs={{0,1},{1,2},{2,3},{3,0},{4,5},{5,6},{6,7},{7,4},{8,9},{9,10},{10,1... | collective-permute-start | bytes 49160 | tf_op jit(solution)/shard_map/ppermute | solution.py:502
  3.0 15.6 %collective-permute-start.1 = (bf16[16,512]{1,0:T(8,128)(2,1)}, bf16[16,512]{1,0:T(8,128)(2,1)S(1)}, u32[]{:S(2)}, u32[]{:S(2)}) collective-permute-start(bf16[16,512]{1,0:T(8,128)(2,1)} %get-tuple-element.23.refs_0_), channel_id=1, source_target_pairs={{0,2},{1,3},{2,0},{3,1},{4,6},{5,7},{6,4},{7,5},{8,10},{9,11},{10,... | collective-permute-start | bytes 49160 | tf_op jit(solution)/shard_map/ppermute | solution.py:502
  4.6 14.1 %collective-permute-start.2 = (bf16[16,512]{1,0:T(8,128)(2,1)}, bf16[16,512]{1,0:T(8,128)(2,1)S(1)}, u32[]{:S(2)}, u32[]{:S(2)}) collective-permute-start(bf16[16,512]{1,0:T(8,128)(2,1)} %get-tuple-element.23.refs_0_), channel_id=1, source_target_pairs={{0,3},{1,0},{2,1},{3,2},{4,7},{5,4},{6,5},{7,6},{8,11},{9,8},{10,9... | collective-permute-start | bytes 49160 | tf_op jit(solution)/shard_map/ppermute | solution.py:502
  18.6 0.6 copy-start.4
  18.6 0.6 copy-start.5
  18.6 0.6 copy-start.6
  19.2 75.8 %copy-start.1 = (bf16[512,512]{1,0:T(8,128)(2,1)S(1)}, bf16[512,512]{1,0:T(8,128)(2,1)}, u32[]{:S(2)}) copy-start(bf16[512,512]{1,0:T(8,128)(2,1)} %refs_0_) | copy-start | bytes 1572868
  95.0 26.2 %collective-permute-start.3 = (bf16[512,512]{1,0:T(8,128)(2,1)S(1)}, bf16[512,512]{1,0:T(8,128)(2,1)S(1)}, u32[]{:S(2)}, u32[]{:S(2)}) collective-permute-start(bf16[512,512]{1,0:T(8,128)(2,1)S(1)} %copy-done.1), channel_id=1, source_target_pairs={{0,1},{1,2},{2,3},{3,0},{4,5},{5,6},{6,7},{7,4},{8,9},{9,10},{10,1... | collective-permute-start | bytes 1572872 | tf_op jit(solution)/shard_map/ppermute | solution.py:502
  95.1 54.8 %collective-permute-start.4 = (bf16[512,512]{1,0:T(8,128)(2,1)S(1)}, bf16[512,512]{1,0:T(8,128)(2,1)S(1)}, u32[]{:S(2)}, u32[]{:S(2)}) collective-permute-start(bf16[512,512]{1,0:T(8,128)(2,1)S(1)} %copy-done.1), channel_id=1, source_target_pairs={{0,2},{1,3},{2,0},{3,1},{4,6},{5,7},{6,4},{7,5},{8,10},{9,11},{10,... | collective-permute-start | bytes 1572872 | tf_op jit(solution)/shard_map/ppermute | solution.py:502
  95.7 54.2 %collective-permute-start.5 = (bf16[512,512]{1,0:T(8,128)(2,1)S(1)}, bf16[512,512]{1,0:T(8,128)(2,1)S(1)}, u32[]{:S(2)}, u32[]{:S(2)}) collective-permute-start(bf16[512,512]{1,0:T(8,128)(2,1)S(1)} %copy-done.1), channel_id=1, source_target_pairs={{0,3},{1,0},{2,1},{3,2},{4,7},{5,4},{6,5},{7,6},{8,11},{9,8},{10,9... | collective-permute-start | bytes 1572872 | tf_op jit(solution)/shard_map/ppermute | solution.py:502
  97.0 23.3 %all-to-all-start = ((bf16[8,16,2048]{2,1,0:T(8,128)(2,1)}), bf16[8,16,2048]{2,1,0:T(8,128)(2,1)S(1)}, u32[]{:S(2)}, u32[]{:S(2)}) async-start(bf16[8,16,2048]{2,1,0:T(8,128)(2,1)} %get-tuple-element.32), calls=%async_computation | async-start | bytes 1048576 | tf_op jit(solution)/shard_map/all_to_all | solution.py:613
  120.5 29.4 %collective-permute-start.6 = (bf16[16,2048]{1,0:T(8,128)(2,1)S(1)}, bf16[16,2048]{1,0:T(8,128)(2,1)S(1)}, u32[]{:S(2)}, u32[]{:S(2)}) collective-permute-start(bf16[16,2048]{1,0:T(8,128)(2,1)S(1)} %reduce_sum.12.refs_4_), channel_id=1, source_target_pairs={{0,1},{1,2},{2,3},{3,0},{4,5},{5,6},{6,7},{7,4},{8,9},{9,10},{10,1... | collective-permute-start | bytes 196616 | tf_op jit(solution)/shard_map/ppermute | solution.py:502
  120.5 29.3 %collective-permute-start.7 = (bf16[16,2048]{1,0:T(8,128)(2,1)S(1)}, bf16[16,2048]{1,0:T(8,128)(2,1)S(1)}, u32[]{:S(2)}, u32[]{:S(2)}) collective-permute-start(bf16[16,2048]{1,0:T(8,128)(2,1)S(1)} %reduce_sum.12.refs_4_), channel_id=1, source_target_pairs={{0,2},{1,3},{2,0},{3,1},{4,6},{5,7},{6,4},{7,5},{8,10},{9,11},{10,... | collective-permute-start | bytes 196616 | tf_op jit(solution)/shard_map/ppermute | solution.py:502
  121.2 28.7 %collective-permute-start.8 = (bf16[16,2048]{1,0:T(8,128)(2,1)S(1)}, bf16[16,2048]{1,0:T(8,128)(2,1)S(1)}, u32[]{:S(2)}, u32[]{:S(2)}) collective-permute-start(bf16[16,2048]{1,0:T(8,128)(2,1)S(1)} %reduce_sum.12.refs_4_), channel_id=1, source_target_pairs={{0,3},{1,0},{2,1},{3,2},{4,7},{5,4},{6,5},{7,6},{8,11},{9,8},{10,9... | collective-permute-start | bytes 196616 | tf_op jit(solution)/shard_map/ppermute | solution.py:502
  122.6 27.3 %copy-start = (bf16[1024,512]{1,0:T(8,128)(2,1)S(1)}, bf16[1024,512]{1,0:T(8,128)(2,1)}, u32[]{:S(2)}) copy-start(bf16[1024,512]{1,0:T(8,128)(2,1)} %in_w_ref.3) | copy-start | bytes 3145732
  122.6 27.3 %copy-start.2 = (bf16[10,1024]{1,0:T(8,128)(2,1)S(1)}, bf16[10,1024]{1,0:T(8,128)(2,1)}, u32[]{:S(2)}) copy-start(bf16[10,1024]{1,0:T(8,128)(2,1)} %embed_ref.3) | copy-start | bytes 61444
  122.6 27.3 %copy-start.3 = (f32[16,512]{1,0:T(8,128)S(1)}, f32[16,512]{1,0:T(8,128)}, u32[]{:S(2)}) copy-start(f32[16,512]{1,0:T(8,128)} %get-tuple-element.31.tanh_ref) | copy-start | bytes 98308
